TPU v7x, 128 devices: a whole 4x4x4 slice. The times are simulated.
128 devices in a mesh: role: 2 (over y_hi), dev: 64 (over z, x, y_lo, core).
Axes of the slice: x: 4, y: 4 (y_hi: 2, y_lo: 2; y = y_hi * 2 + y_lo), z: 4, core: 2. Of those that a mesh axis runs over, the one named last changes fastest.
Arguments:
- tokens: bfloat16 [65536, 1024], P(('role', 'dev')), may hold values from -6 to 6
- expert_ids: int32 [65536, 1], P(('role', 'dev')), may hold values from 0 to 127; in each aligned block of 512 rows (0 to 511, 512 to 1023, ...) at most 8 rows name the same one
- w_qkv: bfloat16 [1024, 3072], P(('role', 'dev')), may hold values from -2 to 2
- w_attn_out: bfloat16 [1024, 1024], P(('role', 'dev')), may hold values from -0.1875 to 0.1875
- gain_attn: bfloat16 [1024], replicated, may hold values from 0.5 to 1.5
- gain_expert: bfloat16 [1024], replicated, may hold values from 0.5 to 1.5
- router: bfloat16 [1024, 128], replicated, may hold values from -0.375 to 0.375
- expert_in: bfloat16 [128, 1024, 2816], P(('role', 'dev')), may hold values from -0.1875 to 0.1875
- expert_out: bfloat16 [128, 2816, 1024], P(('role', 'dev')), may hold values from -0.109375 to 0.109375
- capacity: int32 [128], replicated, may hold values from 256 to 1023
- swap_list: int32 [32], replicated, may hold values from 0 to 63, as said below
Outputs:
- mixed: bfloat16 [65536, 1024], P(('role', 'dev'))
Inputs may be any that keep to these rules, and one draw needn't show every extreme that they name: `expert_ids`: in the rows of one device no expert is named more than 8 times, a bound that some block reaches. `swap_list`: entries are distinct.
All inputs are finite; a program needn't handle non-finite values.
Results may differ from a plain program's by a relative error of at most 0.0052.
Values may be sent and summed in bfloat16 or wider, within the bound.
A program may use at most 128 MiB of HBM per device.

v0:
```python
import jax
import jax.numpy as jnp
from jax import lax
from jax.sharding import PartitionSpec as P

HEADS = 16


def entering(value, axis, join, neutral):
    count, mine = (lax.axis_size(axis), lax.axis_index(axis))
    pieces = lax.all_gather(value, axis)
    total = jnp.full_like(value, 0) + jnp.asarray(neutral, value.dtype)

    def turn(position, total):
        longer = join(total, pieces[position])
        return jnp.where(position < mine, longer, total)

    return lax.fori_loop(0, count - 1, turn, total)


def swapped(value, axis, stride):
    mask = 2**stride
    pairs = [(source, source ^ mask) for source in range(lax.axis_size(axis))]
    return lax.ppermute(value, axis, pairs)


def rms_scale(values, gain_vector):
    mean_sq = jnp.mean(values * values, axis=-1, keepdims=True)
    return values * lax.rsqrt(mean_sq + 1e-06) * gain_vector.astype(jnp.float32)


def self_attend(qkv_rows, head_count):
    row_count = qkv_rows.shape[0]
    model_width = qkv_rows.shape[1] // 3
    head_size = model_width // head_count
    queries = qkv_rows[:, :model_width].reshape(row_count, head_count, head_size)
    keys_all = qkv_rows[:, model_width : 2 * model_width].reshape(row_count, head_count, head_size)
    values = qkv_rows[:, 2 * model_width :].reshape(row_count, head_count, head_size)
    scores = jnp.einsum(
        "shd,thd->hst", queries, keys_all, preferred_element_type=jnp.float32
    ) * head_size ** (-0.5)
    row_max = jnp.max(scores, axis=-1, keepdims=True)
    weights = jnp.exp(scores - row_max)
    soft_weights = (weights / jnp.sum(weights, axis=-1, keepdims=True)).astype(jnp.bfloat16)
    context = jnp.einsum("hst,thd->shd", soft_weights, values, preferred_element_type=jnp.float32)
    return context.reshape(row_count, model_width).astype(jnp.bfloat16)


def add_counts(earlier, later):
    return earlier + later


def shards(
    tokens,
    expert_ids,
    w_qkv,
    w_attn_out,
    gain_attn,
    gain_expert,
    router,
    expert_in,
    expert_out,
    capacity,
    swap_list,
):
    seq_len, model_width = tokens.shape
    residual = tokens.astype(jnp.float32)
    normed = rms_scale(residual, gain_attn).astype(jnp.bfloat16)
    columns = normed
    qkv_rows = jnp.dot(
        columns,
        lax.all_gather(w_qkv, ("role", "dev"), axis=0, tiled=True),
        preferred_element_type=jnp.float32,
    ).astype(jnp.bfloat16)
    context = self_attend(qkv_rows, HEADS)
    columns = context
    attended = jnp.dot(
        columns,
        lax.all_gather(w_attn_out, ("role", "dev"), axis=0, tiled=True),
        preferred_element_type=jnp.float32,
    )
    hidden = residual + attended
    normed_ffn = rms_scale(hidden, gain_expert).astype(jnp.bfloat16)
    logits = jnp.dot(normed_ffn, router, preferred_element_type=jnp.float32)
    experts_all = router.shape[1]
    dev_count = lax.axis_size("dev")
    chosen = expert_ids[:, 0]
    expert_range = jnp.arange(experts_all, dtype=jnp.int32)
    match = chosen[:, None] == expert_range[None, :]
    gate = jax.nn.sigmoid(jnp.sum(jnp.where(match, logits, 0.0), axis=1))
    counts = jnp.sum(match.astype(jnp.int32), axis=0)
    before = entering(counts, ("role", "dev"), add_counts, jnp.zeros_like(counts))
    row_ids = lax.broadcasted_iota(jnp.int32, (seq_len, seq_len), 0)
    col_ids = lax.broadcasted_iota(jnp.int32, (seq_len, seq_len), 1)
    strict_lower = (col_ids < row_ids).astype(jnp.bfloat16)
    rank_table = jnp.dot(
        strict_lower, match.astype(jnp.bfloat16), preferred_element_type=jnp.float32
    )
    local_rank = jnp.sum(jnp.where(match, rank_table, 0.0), axis=1).astype(jnp.int32)
    position = local_rank + jnp.sum(jnp.where(match, before[None, :], 0), axis=1)
    flagged = jnp.any(swap_list[:, None] == jnp.arange(dev_count, dtype=jnp.int32)[None, :], axis=0)
    dev_index = expert_range % dev_count
    role_index = expert_range // dev_count
    flag_expert = jnp.any(
        (dev_index[:, None] == jnp.arange(dev_count, dtype=jnp.int32)[None, :]) & flagged[None, :],
        axis=1,
    )
    location = jnp.where(flag_expert, (1 - role_index) * dev_count + dev_index, expert_range)
    cap_expert = jnp.sum(
        jnp.where(location[:, None] == expert_range[None, :], capacity[None, :], 0), axis=1
    )
    limit = jnp.sum(jnp.where(match, cap_expert[None, :], 0), axis=1)
    kept = position < limit
    slot_rows = max(2, 2 * seq_len // experts_all)
    partner_in, partner_out = swapped((expert_in, expert_out), "role", 0)
    mine_swaps = jnp.any(swap_list == lax.axis_index("dev"))
    weight_in = jnp.where(mine_swaps, partner_in[0], expert_in[0])
    weight_out = jnp.where(mine_swaps, partner_out[0], expert_out[0])
    token_dest = jnp.sum(jnp.where(match, location[None, :], 0), axis=1)
    slot_index = token_dest * slot_rows + local_rank
    buffer = (
        jnp.zeros((experts_all * slot_rows, model_width), jnp.bfloat16)
        .at[slot_index]
        .set(normed_ffn)
    )
    buffer = buffer.reshape(experts_all, slot_rows, model_width)
    received = lax.all_to_all(buffer, ("role", "dev"), split_axis=0, concat_axis=0, tiled=True)
    flat_rows = received.reshape(-1, model_width)
    activ = jnp.maximum(
        jnp.dot(flat_rows, weight_in, preferred_element_type=jnp.float32), 0.0
    ).astype(jnp.bfloat16)
    produced = jnp.dot(activ, weight_out, preferred_element_type=jnp.float32).astype(jnp.bfloat16)
    returned = lax.all_to_all(
        produced.reshape(received.shape), ("role", "dev"), split_axis=0, concat_axis=0, tiled=True
    )
    picked = returned.reshape(-1, model_width)[slot_index].astype(jnp.float32)
    mixed = hidden + jnp.where(kept, gate, 0.0)[:, None] * picked
    return mixed.astype(jnp.bfloat16)


def solution(mesh):
    return jax.shard_map(
        shards,
        mesh=mesh,
        in_specs=(
            P(("role", "dev"), None),
            P(("role", "dev"), None),
            P(("role", "dev"), None),
            P(("role", "dev"), None),
            P(),
            P(),
            P(),
            P(("role", "dev"), None, None),
            P(("role", "dev"), None, None),
            P(),
            P(),
        ),
        out_specs=P(("role", "dev"), None),
        check_vma=False,
    )
```

profile of v0, /device:TPU:1, one launch (start us, length us, event | category | flops | bytes accessed | tf_op | source)
XLA Modules:
  0.0 754.5 jit_solution(13278155795753660415)
XLA Ops:
  6.5 0.0 copy-start
  6.5 0.0 copy-start.6
  6.6 0.0 copy-start.7
  6.6 0.0 all-gather.5.cloned.1.call-start
  6.6 0.7 all-gather.5.cloned.1.call-update
  7.3 0.0 all-gather.7.cloned.1.call-start
  7.3 3.8 collective-permute-start.1
  11.2 0.1 collective-permute-start
  11.3 0.0 all-gather.7.cloned.1.call-update
  11.3 0.8 convert_reduce_fusion
  12.1 1.1 fusion.27
  13.2 1.5 fusion.15
  14.7 412.8 %all-gather.1 = s32[128,1,128]{2,1,0:T(1,128)S(1)} all-gather(s32[1,1,128]{2,1,0:T(1,128)S(1)} %bitcast.57), channel_id=2, replica_groups=mesh['role'=2,'dev'=64] {'role','dev'}, dimensions={0}, use_global_device_ids=true | all-gather | bytes 66048 | tf_op jit(solution)/shard_map/all_gather | solution.py:11
  427.5 5.1 while.14
  432.7 0.0 copy-done.9
  432.7 0.1 fusion.36
  432.8 0.1 fusion.35
  432.9 0.0 copy-done.8
  432.9 0.2 select_reduce_fusion.3
  433.1 0.0 copy-done.5
  433.1 0.1 select_reduce_fusion.2
  433.2 0.0 copy-done.6
  433.3 0.0 copy-done.7
  433.3 16.4 %all-gather.5.cloned.1.call-done = bf16[1024,3072]{1,0:T(8,128)(2,1)} async-done(((bf16[8,3072]{1,0:T(8,128)(2,1)}), bf16[1024,3072]{1,0:T(8,128)(2,1)}) %all-gather.5.cloned.1.call-update) | async-done | bytes 6291472 | tf_op jit(solution)/shard_map/all_gather | solution.py:72
  449.7 0.0 copy-done.2
  449.7 6.6 convolution_convert_fusion
  456.2 1.3 fusion.43
  457.5 2.3 copy.24
  459.8 1.3 copy.25
  461.1 1.3 copy.26
  462.4 10.1 %fusion.44 = (f32[16,512]{1,0:T(8,128)S(1)}, f32[16,512,512]{1,2,0:T(8,128)}) fusion(bf16[512,16,64]{0,2,1:T(8,128)(2,1)S(1)} %bitcast.46, bf16[512,16,64]{0,2,1:T(8,128)(2,1)} %bitcast.47), kind=kOutput, calls=%fused_computation.75 | convolution fusion | flops 549454336 | bytes 18907136 | tf_op jit(solution)/shard_map/sub | solution.py:43
  472.5 0.0 copy-done.3
  472.5 8.3 %fusion.21 = bf16[16,64,512]{2,1,0:T(8,128)(2,1)} fusion(bf16[512,16,64]{0,2,1:T(8,128)(2,1)S(1)} %bitcast.45, f32[16,512,512]{1,2,0:T(8,128)} %get-tuple-element.115, f32[16,512]{1,0:T(8,128)S(1)} %get-tuple-element.114), kind=kOutput, calls=%fused_computation.32 | convolution fusion | flops 545783808 | bytes 18907136 | tf_op jit(solution)/shard_map/hst,thd->shd/dot_general | solution.py:45
  480.8 163.3 %all-gather.7.cloned.1.call-done = bf16[1024,1024]{1,0:T(8,128)(2,1)} async-done(((bf16[8,1024]{1,0:T(8,128)(2,1)}), bf16[1024,1024]{1,0:T(8,128)(2,1)}) %all-gather.7.cloned.1.call-update) | async-done | bytes 2097168 | tf_op jit(solution)/shard_map/all_gather | solution.py:79
  644.2 3.3 multiply_reduce_fusion.1
  647.5 4.2 scatter_custom_fusion
  651.7 0.0 copy-done.1
  651.7 7.1 all-to-all-start
  658.7 0.6 compare_reduce_fusion
  659.4 0.0 collective-permute-done.1
  659.4 0.0 collective-permute-done
  659.4 29.5 %all-to-all-done = bf16[128,8,1024]{2,1,0:T(8,128)(2,1)S(1)} async-done(((bf16[128,8,1024]{2,1,0:T(8,128)(2,1)}), bf16[128,8,1024]{2,1,0:T(8,128)(2,1)S(1)}, u32[]{:S(2)}, u32[]{:S(2)}) %all-to-all-start) | async-done | bytes 2097184 | tf_op jit(solution)/shard_map/all_to_all | solution.py:127
  688.9 18.3 %convert_bitcast_fusion = bf16[128,8,1024]{2,1,0:T(8,128)(2,1)} fusion(bf16[1,2816,1024]{2,1,0:T(8,128)(2,1)} %collective-permute-done.1, bf16[1,2816,1024]{2,1,0:T(8,128)(2,1)} %param.21, pred[]{:T(512)} %compare_reduce_fusion, bf16[1,1024,2816]{2,1,0:T(8,128)(2,1)} %collective-permute-done, bf16[1,1024,2816]{2,1,0:T(8,128)(2,1)} %param.20, ...), kind=kOutput, calls=%fused_computation.29 | convolution fusion | flops 11823742976 | bytes 27262976 | tf_op jit(solution)/shard_map/dot_general | solution.py:132
  707.2 5.4 all-to-all-start.1
  712.7 2.2 fusion.26
  714.9 27.9 %all-to-all-done.1 = bf16[128,8,1024]{2,1,0:T(8,128)(2,1)S(1)} async-done(((bf16[128,8,1024]{2,1,0:T(8,128)(2,1)}), bf16[128,8,1024]{2,1,0:T(8,128)(2,1)S(1)}, u32[]{:S(2)}, u32[]{:S(2)}) %all-to-all-start.1) | async-done | bytes 2097184 | tf_op jit(solution)/shard_map/all_to_all | solution.py:133
  742.8 2.0 gather_fusion
  744.8 2.9 add_convert_fusion
  (147 shorter events, 2.3 us)
Async XLA Ops:
  6.5 706.1 %copy-start = (bf16[1024,128]{1,0:T(8,128)(2,1)S(1)}, bf16[1024,128]{1,0:T(8,128)(2,1)}, u32[]{:S(2)}) copy-start(bf16[1024,128]{1,0:T(8,128)(2,1)} %param.19) | copy-start | bytes 786436
  6.5 426.5 %copy-start.5 = (s32[512,1]{0,1:T(1,128)S(1)}, s32[512,1]{0,1:T(1,128)}, u32[]{:S(2)}) copy-start(s32[512,1]{0,1:T(1,128)} %param.14) | copy-start | bytes 6148
  6.5 443.1 %copy-start.2 = (bf16[512,1024]{1,0:T(8,128)(2,1)S(1)}, bf16[512,1024]{1,0:T(8,128)(2,1)}, u32[]{:S(2)}) copy-start(bf16[512,1024]{1,0:T(8,128)(2,1)} %param.13) | copy-start | bytes 3145732
  6.5 426.1 %copy-start.9 = (s32[32]{0:T(128)S(1)}, s32[32]{0:T(128)}, u32[]{:S(2)}) copy-start(s32[32]{0:T(128)} %param.23) | copy-start | bytes 388
  6.5 426.3 %copy-start.8 = (s32[128]{0:T(128)S(1)}, s32[128]{0:T(128)}, u32[]{:S(2)}) copy-start(s32[128]{0:T(128)} %param.22) | copy-start | bytes 1540
  6.5 426.7 %copy-start.6 = (bf16[1024]{0:T(1024)(128)(2,1)S(1)}, bf16[1024]{0:T(1024)(128)(2,1)}, u32[]{:S(2)}) copy-start(bf16[1024]{0:T(1024)(128)(2,1)} %param.17) | copy-start | bytes 6148
  6.6 426.7 %copy-start.7 = (bf16[1024]{0:T(1024)(128)(2,1)S(1)}, bf16[1024]{0:T(1024)(128)(2,1)}, u32[]{:S(2)}) copy-start(bf16[1024]{0:T(1024)(128)(2,1)} %param.18) | copy-start | bytes 6148
  6.6 443.1 %all-gather.5.cloned.1.call-start = ((), (), s32[]{:S(2)}) async-start(), calls=%async_computation.2 | async-start | bytes 6340608 | tf_op jit(solution)/shard_map/all_gather | solution.py:72
  7.3 636.9 %all-gather.7.cloned.1.call-start = ((), (), s32[]{:S(2)}) async-start(), calls=%async_computation.3 | async-start | bytes 2113536 | tf_op jit(solution)/shard_map/all_gather | solution.py:79
  7.3 652.0 %collective-permute-start.1 = (bf16[1,2816,1024]{2,1,0:T(8,128)(2,1)}, bf16[1,2816,1024]{2,1,0:T(8,128)(2,1)}, u32[]{:S(2)}, u32[]{:S(2)}) collective-permute-start(bf16[1,2816,1024]{2,1,0:T(8,128)(2,1)} %param.21), channel_id=1, source_target_pairs={{0,64},{64,0},{1,65},{65,1},{2,66},{66,2},{3,67},{67,3},{4,68},{68... | collective-permute-start | bytes 17301512 | tf_op jit(solution)/shard_map/ppermute | solution.py:24
  11.2 648.2 %collective-permute-start = (bf16[1,1024,2816]{2,1,0:T(8,128)(2,1)}, bf16[1,1024,2816]{2,1,0:T(8,128)(2,1)}, u32[]{:S(2)}, u32[]{:S(2)}) collective-permute-start(bf16[1,1024,2816]{2,1,0:T(8,128)(2,1)} %param.20), channel_id=1, source_target_pairs={{0,64},{64,0},{1,65},{65,1},{2,66},{66,2},{3,67},{67,3},{4,68},{68... | collective-permute-start | bytes 17301512 | tf_op jit(solution)/shard_map/ppermute | solution.py:24
  461.1 1.3 copy-start.4
  462.4 10.1 %copy-start.3 = (bf16[512,1024]{0,1:T(8,128)(2,1)S(1)}, bf16[512,1024]{0,1:T(8,128)(2,1)}, u32[]{:S(2)}) copy-start(bf16[512,1024]{0,1:T(8,128)(2,1)} %copy.24) | copy-start | bytes 3145732
  647.4 4.2 copy-start.1
  651.7 37.2 %all-to-all-start = ((bf16[128,8,1024]{2,1,0:T(8,128)(2,1)}), bf16[128,8,1024]{2,1,0:T(8,128)(2,1)S(1)}, u32[]{:S(2)}, u32[]{:S(2)}) async-start(bf16[128,8,1024]{2,1,0:T(8,128)(2,1)} %bitcast.44), calls=%async_computation | async-start | bytes 4194304 | tf_op jit(solution)/shard_map/all_to_all | solution.py:127
  707.2 35.6 %all-to-all-start.1 = ((bf16[128,8,1024]{2,1,0:T(8,128)(2,1)}), bf16[128,8,1024]{2,1,0:T(8,128)(2,1)S(1)}, u32[]{:S(2)}, u32[]{:S(2)}) async-start(bf16[128,8,1024]{2,1,0:T(8,128)(2,1)} %convert_bitcast_fusion), calls=%async_computation.1 | async-start | bytes 4194304 | tf_op jit(solution)/shard_map/all_to_all | solution.py:133
Sparse Core Ops, SparseCore 0:
  9.1 440.4 all-gather.4
  451.4 192.7 all-gather.6
where the time goes:
time: 755 us
  blocking collectives  413 us (55%)
  waiting for transfers between devices  238 us (32%)
  matrix products  49.8 us (7%)
  starting transfers between devices  16.5 us (2%)
  between operations  13.6 us (2%)
  other arithmetic  12.8 us (2%)
  local copies, waits for them, and re-layouts  8.29 us (1%)
    all_gather x1, blocking collectives, entering(): pieces = lax.all_gather(value, axis)  413 us
    all_gather x1, waiting for transfers between devices, shards(): lax.all_gather(w_attn_out, ('role', 'dev'), axis=0, tiled=True)  163 us
    all_to_all x1, waiting for transfers between devices, shards(): lax.all_to_all(buffer, ('role', 'dev'), split_axis=0, concat_axis=0, tile...  29.5 us
    all_to_all x1, waiting for transfers between devices, shards(): lax.all_to_all(produced.reshape(received.shape), ('role', 'dev'), split_a...  27.9 us
    dot_general x1, matrix products, shards(): jnp.dot(activ, weight_out, preferred_element_type=jnp.float32)  18.3 us
    all_gather x1, waiting for transfers between devices, shards(): lax.all_gather(w_qkv, ('role', 'dev'), axis=0, tiled=True)  16.4 us
  transfers between devices with their start and end apart: 6, of which 4 were waited for; matrix products, arithmetic and copies ran while one was open for 6% of the time, Pallas kernels for 0%

commit v1 on v0

v1 whole, which is shorter than its diff:
```python
import jax
import jax.numpy as jnp
from jax import lax
from jax.sharding import PartitionSpec as P

HEADS = 16


def rms_scale(values, gain_vector):
    mean_sq = jnp.mean(values * values, axis=-1, keepdims=True)
    return values * lax.rsqrt(mean_sq + 1e-06) * gain_vector.astype(jnp.float32)


def self_attend(qkv_rows, head_count):
    row_count = qkv_rows.shape[0]
    model_width = qkv_rows.shape[1] // 3
    head_size = model_width // head_count
    queries = qkv_rows[:, :model_width].reshape(row_count, head_count, head_size)
    keys_all = qkv_rows[:, model_width : 2 * model_width].reshape(row_count, head_count, head_size)
    values = qkv_rows[:, 2 * model_width :].reshape(row_count, head_count, head_size)
    scores = jnp.einsum(
        "shd,thd->hst", queries, keys_all, preferred_element_type=jnp.float32
    ) * head_size ** (-0.5)
    row_max = jnp.max(scores, axis=-1, keepdims=True)
    weights = jnp.exp(scores - row_max)
    soft_weights = (weights / jnp.sum(weights, axis=-1, keepdims=True)).astype(jnp.bfloat16)
    context = jnp.einsum("hst,thd->shd", soft_weights, values, preferred_element_type=jnp.float32)
    return context.reshape(row_count, model_width).astype(jnp.bfloat16)


def shards(
    tokens,
    expert_ids,
    w_qkv,
    w_attn_out,
    gain_attn,
    gain_expert,
    router,
    expert_in,
    expert_out,
    capacity,
    swap_list,
):
    seq_len, model_width = tokens.shape
    experts_all = router.shape[1]
    dev_count = lax.axis_size("dev")
    me = lax.axis_index("role") * dev_count + lax.axis_index("dev")
    chosen = expert_ids[:, 0]
    expert_range = jnp.arange(experts_all, dtype=jnp.int32)
    match = chosen[:, None] == expert_range[None, :]
    counts = jnp.sum(match.astype(jnp.float32), axis=0)
    row_share = w_attn_out.shape[0]
    beside = jnp.broadcast_to(counts.astype(jnp.bfloat16)[None, :], (row_share, experts_all))
    w_qkv_all = lax.all_gather(w_qkv, ("role", "dev"), axis=0, tiled=True)
    w_out_counts = lax.all_gather(
        jnp.concatenate([w_attn_out, beside], axis=1), ("role", "dev"), axis=0, tiled=True
    )
    w_out_all = w_out_counts[:, :model_width]
    counts_all = w_out_counts[:, model_width:].astype(jnp.float32)
    residual = tokens.astype(jnp.float32)
    normed = rms_scale(residual, gain_attn).astype(jnp.bfloat16)
    qkv_rows = jnp.dot(normed, w_qkv_all, preferred_element_type=jnp.float32).astype(jnp.bfloat16)
    context = self_attend(qkv_rows, HEADS)
    attended = jnp.dot(context, w_out_all, preferred_element_type=jnp.float32)
    hidden = residual + attended
    normed_ffn = rms_scale(hidden, gain_expert).astype(jnp.bfloat16)
    logits = jnp.dot(normed_ffn, router, preferred_element_type=jnp.float32)
    gate = jax.nn.sigmoid(jnp.sum(jnp.where(match, logits, 0.0), axis=1))
    gathered_row = jnp.arange(w_out_counts.shape[0], dtype=jnp.int32)
    first_of_lower = (gathered_row % row_share == 0) & (gathered_row < me * row_share)
    before = jnp.sum(jnp.where(first_of_lower[:, None], counts_all, 0.0), axis=0).astype(jnp.int32)
    row_ids = lax.broadcasted_iota(jnp.int32, (seq_len, seq_len), 0)
    col_ids = lax.broadcasted_iota(jnp.int32, (seq_len, seq_len), 1)
    strict_lower = (col_ids < row_ids).astype(jnp.bfloat16)
    rank_table = jnp.dot(
        strict_lower, match.astype(jnp.bfloat16), preferred_element_type=jnp.float32
    )
    local_rank = jnp.sum(jnp.where(match, rank_table, 0.0), axis=1).astype(jnp.int32)
    flagged = jnp.any(
        swap_list[:, None] == (expert_range % dev_count)[None, :], axis=0
    )
    location = jnp.where(
        flagged, (1 - expert_range // dev_count) * dev_count + expert_range % dev_count, expert_range
    )
    cap_expert = jnp.sum(
        jnp.where(location[:, None] == expert_range[None, :], capacity[None, :], 0), axis=1
    )
    room = jnp.sum(jnp.where(match, (cap_expert - before)[None, :], 0), axis=1)
    kept = local_rank < room
    slot_rows = max(2, 2 * seq_len // experts_all)
    slot_index = chosen * slot_rows + local_rank
    buffer = (
        jnp.zeros((experts_all * slot_rows, model_width), jnp.bfloat16)
        .at[slot_index]
        .set(normed_ffn)
    )
    buffer = buffer.reshape(experts_all, slot_rows, model_width)
    received = lax.all_to_all(buffer, ("role", "dev"), split_axis=0, concat_axis=0, tiled=True)
    flat_rows = received.reshape(-1, model_width)
    activ = jnp.maximum(
        jnp.dot(flat_rows, expert_in[0], preferred_element_type=jnp.float32), 0.0
    ).astype(jnp.bfloat16)
    produced = jnp.dot(activ, expert_out[0], preferred_element_type=jnp.float32).astype(jnp.bfloat16)
    returned = lax.all_to_all(
        produced.reshape(received.shape), ("role", "dev"), split_axis=0, concat_axis=0, tiled=True
    )
    picked = returned.reshape(-1, model_width)[slot_index].astype(jnp.float32)
    mixed = hidden + jnp.where(kept, gate, 0.0)[:, None] * picked
    return mixed.astype(jnp.bfloat16)


def solution(mesh):
    return jax.shard_map(
        shards,
        mesh=mesh,
        in_specs=(
            P(("role", "dev"), None),
            P(("role", "dev"), None),
            P(("role", "dev"), None),
            P(("role", "dev"), None),
            P(),
            P(),
            P(),
            P(("role", "dev"), None, None),
            P(("role", "dev"), None, None),
            P(),
            P(),
        ),
        out_specs=P(("role", "dev"), None),
        check_vma=False,
    )
```

time: 755 us -> 544 us (0.72)
  blocking collectives: 413 us -> 37.2 us
  waiting for transfers between devices: 238 us -> 424 us
  starting transfers between devices: 16.5 us -> 5.47 us
    all_gather x1 -> x0, blocking collectives: 413 us -> none  [entering(): pieces = lax.all_gather(value, axis)]
    all_gather x2, waiting for transfers between devices: 180 us -> 393 us  [the longest x1 200 us: shards(): w_qkv_all = lax.all_gather(w_qkv, ('role', 'dev'), axis=0, tiled=True)]
    all_to_all x0 -> x1, blocking collectives: none -> 37.2 us  [shards(): lax.all_to_all(buffer, ('role', 'dev'), split_axis=0, concat_axis=0, tile...]
    all_to_all x1 -> x0, waiting for transfers between devices: 29.5 us -> none  [shards(): lax.all_to_all(buffer, ('role', 'dev'), split_axis=0, concat_axis=0, tile...]
  transfers between devices with their start and end apart: 6 -> 3, of which waited for: 4 -> 3; matrix products, arithmetic and copies ran while one was open for 6% -> 1% of each run, Pallas kernels for 0% -> 0%
where the time goes in v1:
time: 544 us
  waiting for transfers between devices  424 us (78%)
  matrix products  43.8 us (8%)
  blocking collectives  37.2 us (7%)
  other arithmetic  15.1 us (3%)
  between operations  13.6 us (2%)
  starting transfers between devices  5.47 us (1%)
    all_gather x1, waiting for transfers between devices, shards(): w_qkv_all = lax.all_gather(w_qkv, ('role', 'dev'), axis=0, tiled=True)  200 us
    all_gather x1, waiting for transfers between devices, shards(): lax.all_gather(jnp.concatenate([w_attn_out, beside], axis=1), ('role', 'd...  193 us
    all_to_all x1, blocking collectives, shards(): lax.all_to_all(buffer, ('role', 'dev'), split_axis=0, concat_axis=0, tile...  37.2 us
    all_to_all x1, waiting for transfers between devices, shards(): lax.all_to_all(produced.reshape(received.shape), ('role', 'dev'), split_a...  30.1 us
    dot_general x1, matrix products, shards(): jnp.dot(activ, expert_out[0], preferred_element_type=jnp.float32)  17.7 us
  transfers between devices with their start and end apart: 3, of which 3 were waited for; matrix products, arithmetic and copies ran while one was open for 1% of the time, Pallas kernels for 0%

profile of v1, /device:TPU:1, one launch (start us, length us, event | category | flops | bytes accessed | tf_op | source)
XLA Modules:
  0.0 543.9 jit_solution(13328983588783734657)
XLA Ops:
  6.5 0.0 copy-start
  6.5 0.0 copy-start.5
  6.5 0.0 copy-start.2
  6.5 0.0 all-gather.5.cloned.1.call-start
  6.5 0.9 convert_reduce_fusion
  7.5 1.3 pad_maximum_fusion
  8.8 0.0 all-gather.5.cloned.1.call-update
  8.8 0.0 all-gather.3.cloned.1.call-start
  8.9 0.7 all-gather.3.cloned.1.call-update
  9.6 0.7 convert_element_type.81
  10.3 0.7 convert_element_type.93
  11.0 0.7 compare_reduce_fusion
  11.7 0.8 select_reduce_fusion.2
  12.5 1.1 fusion.30
  13.6 1.5 fusion.13
  15.1 192.9 %all-gather.5.cloned.1.call-done = bf16[1024,1152]{1,0:T(8,128)(2,1)} async-done(((bf16[8,1152]{1,0:T(8,128)(2,1)}), bf16[1024,1152]{1,0:T(8,128)(2,1)}) %all-gather.5.cloned.1.call-update) | async-done | bytes 2359312 | tf_op jit(solution)/shard_map/all_gather | solution.py:55
  208.1 1.2 select_reduce_fusion
  209.2 0.0 copy-done.5
  209.3 0.1 select_reduce_fusion.1
  209.4 200.2 %all-gather.3.cloned.1.call-done = bf16[1024,3072]{1,0:T(8,128)(2,1)} async-done(((bf16[8,3072]{1,0:T(8,128)(2,1)}), bf16[1024,3072]{1,0:T(8,128)(2,1)}) %all-gather.3.cloned.1.call-update) | async-done | bytes 6291472 | tf_op jit(solution)/shard_map/all_gather | solution.py:54
  409.6 0.0 copy-done.2
  409.6 6.6 %convolution_convert_fusion = bf16[512,3072]{1,0:T(8,128)(2,1)S(1)} fusion(bf16[1024,3072]{1,0:T(8,128)(2,1)} %all-gather.3.cloned.1.call-done, bf16[512,1024]{1,0:T(8,128)(2,1)S(1)} %copy-done.2, f32[1024]{0:T(1024)S(1)} %convert_element_type.81, f32[512]{0:T(512)S(1)} %add_rsqrt_fusion.1), kind=kOutput, calls=%fused_computation.13 | convolution fusion | flops 3224895488 | bytes 10491904 | tf_op jit(solution)/shard_map/dot_general | solution.py:62
  416.2 0.3 fusion.48
  416.5 1.3 copy.20
  417.8 0.5 copy.21
  418.4 0.5 copy.22
  418.9 0.0 copy-start.4
  418.9 8.9 %fusion.49 = (f32[16,512]{1,0:T(8,128)S(1)}, f32[16,512,512]{1,2,0:T(8,128)}) fusion(bf16[512,16,64]{0,2,1:T(8,128)(2,1)S(1)} %bitcast.42, bf16[512,16,64]{0,2,1:T(8,128)(2,1)S(1)} %bitcast.43), kind=kOutput, calls=%fused_computation.73 | convolution fusion | flops 549454336 | bytes 18907136 | tf_op jit(solution)/shard_map/sub | solution.py:25
  427.8 0.0 copy-done.4
  427.8 0.0 copy-start.3
  427.9 0.0 copy-start.6
  427.9 7.6 %fusion.28 = bf16[16,64,512]{2,1,0:T(8,128)(2,1)S(1)} fusion(bf16[512,16,64]{0,2,1:T(8,128)(2,1)S(1)} %bitcast.41, f32[16,512,512]{1,2,0:T(8,128)} %get-tuple-element.11, f32[16,512]{1,0:T(8,128)S(1)} %get-tuple-element.10), kind=kOutput, calls=%fused_computation.28 | convolution fusion | flops 545783808 | bytes 18907136 | tf_op jit(solution)/shard_map/hst,thd->shd/dot_general | solution.py:27
  435.4 0.0 copy-done.3
  435.5 0.0 copy-done.6
  435.5 1.4 multiply_reduce_fusion.1
  436.8 0.0 copy-start.1
  436.9 0.0 copy-done
  436.9 0.6 fusion.29
  437.5 4.2 scatter_custom_fusion
  441.7 0.0 copy-done.1
  441.7 37.2 %all_to_all.10 = bf16[128,8,1024]{2,1,0:T(8,128)(2,1)S(1)} all-to-all(bf16[128,8,1024]{2,1,0:T(8,128)(2,1)} %bitcast.40), channel_id=1, replica_groups=mesh['role'=2,'dev'=64] {'role','dev'}, dimensions={0} | all-to-all | bytes 4194304 | tf_op jit(solution)/shard_map/all_to_all | solution.py:98
  478.9 17.7 %convert_bitcast_fusion = bf16[128,8,1024]{2,1,0:T(8,128)(2,1)} fusion(bf16[1,2816,1024]{2,1,0:T(8,128)(2,1)} %param.19, bf16[1,1024,2816]{2,1,0:T(8,128)(2,1)} %param.18, bf16[128,8,1024]{2,1,0:T(8,128)(2,1)S(1)} %all_to_all.10), kind=kOutput, calls=%fused_computation.25 | convolution fusion | flops 11817975808 | bytes 15728640 | tf_op jit(solution)/shard_map/dot_general | solution.py:103
  496.6 5.4 all-to-all-start.1
  502.0 30.1 %all-to-all-done.1 = bf16[128,8,1024]{2,1,0:T(8,128)(2,1)S(1)} async-done(((bf16[128,8,1024]{2,1,0:T(8,128)(2,1)}), bf16[128,8,1024]{2,1,0:T(8,128)(2,1)S(1)}, u32[]{:S(2)}, u32[]{:S(2)}) %all-to-all-start.1) | async-done | bytes 2097184 | tf_op jit(solution)/shard_map/all_to_all | solution.py:104
  532.1 2.0 gather_fusion
  534.2 2.9 add_convert_fusion
  (10 shorter events, 0.1 us)
Async XLA Ops:
  6.5 430.3 %copy-start = (bf16[1024,128]{1,0:T(8,128)(2,1)S(1)}, bf16[1024,128]{1,0:T(8,128)(2,1)}, u32[]{:S(2)}) copy-start(bf16[1024,128]{1,0:T(8,128)(2,1)} %param.17) | copy-start | bytes 786436
  6.5 202.7 %copy-start.5 = (s32[512,1]{0,1:T(1,128)S(1)}, s32[512,1]{0,1:T(1,128)}, u32[]{:S(2)}) copy-start(s32[512,1]{0,1:T(1,128)} %param.12) | copy-start | bytes 6148
  6.5 403.0 %copy-start.2 = (bf16[512,1024]{1,0:T(8,128)(2,1)S(1)}, bf16[512,1024]{1,0:T(8,128)(2,1)}, u32[]{:S(2)}) copy-start(bf16[512,1024]{1,0:T(8,128)(2,1)} %param.11) | copy-start | bytes 3145732
  6.5 201.5 %all-gather.5.cloned.1.call-start = ((), (), s32[]{:S(2)}) async-start(), calls=%async_computation.3 | async-start | bytes 2377728 | tf_op jit(solution)/shard_map/all_gather | solution.py:55
  8.8 400.8 %all-gather.3.cloned.1.call-start = ((), (), s32[]{:S(2)}) async-start(), calls=%async_computation.2 | async-start | bytes 6340608 | tf_op jit(solution)/shard_map/all_gather | solution.py:54
  418.9 8.9 %copy-start.4 = (bf16[512,1024]{0,1:T(8,128)(2,1)S(1)}, bf16[512,1024]{0,1:T(8,128)(2,1)}, u32[]{:S(2)}) copy-start(bf16[512,1024]{0,1:T(8,128)(2,1)} %copy.20) | copy-start | bytes 3145732
  427.8 7.6 %copy-start.3 = (bf16[512,1024]{1,0:T(8,128)(2,1)S(1)}, bf16[512,1024]{1,0:T(8,128)(2,1)}, u32[]{:S(2)}) copy-start(bf16[512,1024]{1,0:T(8,128)(2,1)} %param.11) | copy-start | bytes 3145732
  427.9 7.6 %copy-start.6 = (bf16[1024,1152]{1,0:T(8,128)(2,1)S(1)}, bf16[1024,1152]{1,0:T(8,128)(2,1)}, u32[]{:S(2)}) copy-start(bf16[1024,1152]{1,0:T(8,128)(2,1)} %all-gather.5.cloned.1.call-done) | copy-start | bytes 7077892
  436.8 4.9 copy-start.1
  496.6 35.6 %all-to-all-start.1 = ((bf16[128,8,1024]{2,1,0:T(8,128)(2,1)}), bf16[128,8,1024]{2,1,0:T(8,128)(2,1)S(1)}, u32[]{:S(2)}, u32[]{:S(2)}) async-start(bf16[128,8,1024]{2,1,0:T(8,128)(2,1)} %convert_bitcast_fusion), calls=%async_computation.1 | async-start | bytes 4194304 | tf_op jit(solution)/shard_map/all_to_all | solution.py:104
Sparse Core Ops, SparseCore 0:
  9.1 198.9 all-gather.4
  209.8 199.7 all-gather.2

commit v2 on v1

--- a/solution.py
+++ b/solution.py
@@ -1,9 +1,129 @@
 import jax
 import jax.numpy as jnp
 from jax import lax
+from jax.experimental import pallas as pl
+from jax.experimental.pallas import tpu as pltpu
 from jax.sharding import PartitionSpec as P
 
 HEADS = 16
+MESH = pl.DeviceIdType.MESH
+
+def coordinates():
+    role, dev = lax.axis_index("role"), lax.axis_index("dev")
+    return {"z": dev // 16, "x": dev // 4 % 4, "y": role * 2 + dev // 2 % 2, "core": dev % 2}
+
+def device_of(at):
+    y = at["y"]
+    return (y // 2, ((at["z"] * 4 + at["x"]) * 2 + y % 2) * 2 + at["core"])
+
+def moved(at, axis, by):
+    size = 2 if axis == "core" else 4
+    return {**at, axis: (at[axis] + by) % size}
+
+def block_of(buf, at, whole, cols):
+    every = slice(None)
+    yh, yl = (every, every) if "y" in whole else (at["y"] // 2, at["y"] % 2)
+    z = every if "z" in whole else at["z"]
+    x = every if "x" in whole else at["x"]
+    return buf.at[yh, z, x, yl, at["core"], every, slice(*cols)]
+
+ORDERS = (("z", "x", "y"), ("x", "y", "z"), ("y", "z", "x"))
+
+class Gather:
+    def __init__(self, buf, cols, order, at, send, recv, first):
+        self.buf, self.cols, self.order, self.at = buf, cols, order, at
+        self.send, self.recv, self.first = send, recv, first
+        self.started = []
+        span = (cols[1] - cols[0]) // 128
+        mid = cols[0] + (span // 2) * 128
+        self.halves = ((cols[0], mid), (mid, cols[1]))
+
+    def copy(self, block_at, whole, cols, to, slot):
+        ref = block_of(self.buf, block_at, whole, cols)
+        return pltpu.make_async_remote_copy(
+            src_ref=ref, dst_ref=ref, send_sem=self.send.at[self.first + slot],
+            recv_sem=self.recv.at[self.first + slot], device_id=device_of(to), device_id_type=MESH)
+
+    def start(self, *args):
+        copy = self.copy(*args)
+        copy.start()
+        self.started.append(copy)
+
+    def whole(self, phase):
+        return self.order[:phase]
+
+    def open_phase(self, phase):
+        axis, whole = self.order[phase], self.whole(phase)
+        self.start(self.at, whole, self.cols, moved(self.at, axis, 1), phase * 4)
+        self.start(self.at, whole, self.cols, moved(self.at, axis, 3), phase * 4 + 1)
+        if phase == 2:
+            self.start(self.at, whole, self.cols, moved(self.at, "core", 1), 12)
+
+    def turn_phase(self, phase):
+        axis, whole = self.order[phase], self.whole(phase)
+        left, right = moved(self.at, axis, 3), moved(self.at, axis, 1)
+        self.copy(left, whole, self.cols, left, phase * 4).wait_recv()
+        self.start(left, whole, self.halves[0], right, phase * 4 + 2)
+        self.copy(right, whole, self.cols, right, phase * 4 + 1).wait_recv()
+        self.start(right, whole, self.halves[1], left, phase * 4 + 3)
+        if phase == 2:
+            other = moved(self.at, "core", 1)
+            self.start(left, whole, self.cols, other, 13)
+            self.start(right, whole, self.cols, other, 14)
+
+    def close_phase(self, phase):
+        axis, whole = self.order[phase], self.whole(phase)
+        left, right = moved(self.at, axis, 3), moved(self.at, axis, 1)
+        far = moved(self.at, axis, 2)
+        self.copy(far, whole, self.halves[0], left, phase * 4 + 2).wait_recv()
+        self.copy(far, whole, self.halves[1], right, phase * 4 + 3).wait_recv()
+        if phase == 2:
+            self.start(far, whole, self.cols, moved(self.at, "core", 1), 15)
+
+    def finish(self):
+        axis, whole = self.order[2], self.whole(2)
+        other = moved(self.at, "core", 1)
+        for slot, by in ((12, 0), (13, 3), (14, 1), (15, 2)):
+            self.copy(moved(other, axis, by), whole, self.cols, other, slot).wait_recv()
+
+    def drain(self):
+        for copy in self.started:
+            copy.wait_send()
+
+def greet(at):
+    barrier = pltpu.get_barrier_semaphore()
+    for axis, by in (("z", 1), ("z", 3), ("x", 1), ("x", 3), ("y", 1), ("y", 3), ("core", 1)):
+        pl.semaphore_signal(barrier, inc=1, device_id=device_of(moved(at, axis, by)), device_id_type=MESH)
+    pl.semaphore_wait(barrier, 7)
+
+def gather_kernel(qkv_ref, out_ref, qkv_all, out_all, send, recv):
+    at = coordinates()
+    own = (at["y"] // 2, at["z"], at["x"], at["y"] % 2, at["core"])
+    qkv_all[own] = qkv_ref[...]
+    out_all[own] = out_ref[...]
+    greet(at)
+    pieces = []
+    for buf, third in ((qkv_all, qkv_ref.shape[1] // 3), (out_all, out_ref.shape[1] // 3)):
+        for n, order in enumerate(ORDERS):
+            pieces.append(Gather(buf, (n * third, (n + 1) * third), order, at, send, recv, 16 * len(pieces)))
+    for phase in range(3):
+        for piece in pieces: piece.open_phase(phase)
+        for piece in pieces: piece.turn_phase(phase)
+        for piece in pieces: piece.close_phase(phase)
+    for piece in pieces: piece.finish()
+    for piece in pieces: piece.drain()
+
+def gather(w_qkv, w_out):
+    lead = (2, 4, 4, 2, 2)
+    return pl.pallas_call(
+        gather_kernel,
+        out_shape=[jax.ShapeDtypeStruct(lead + w_qkv.shape, w_qkv.dtype), jax.ShapeDtypeStruct(lead + w_out.shape, w_out.dtype)],
+        in_specs=[pl.BlockSpec(memory_space=pltpu.VMEM)] * 2,
+        out_specs=[pl.BlockSpec(memory_space=pltpu.VMEM)] * 2,
+        scratch_shapes=[pltpu.SemaphoreType.DMA((96,)), pltpu.SemaphoreType.DMA((96,))],
+        compiler_params=pltpu.CompilerParams(collective_id=0, has_side_effects=True, vmem_limit_bytes=40 << 20),
+        name="gather_weights",
+    )(w_qkv, w_out)
 
 
 def rms_scale(values, gain_vector):
@@ -51,10 +171,9 @@
     counts = jnp.sum(match.astype(jnp.float32), axis=0)
     row_share = w_attn_out.shape[0]
     beside = jnp.broadcast_to(counts.astype(jnp.bfloat16)[None, :], (row_share, experts_all))
-    w_qkv_all = lax.all_gather(w_qkv, ("role", "dev"), axis=0, tiled=True)
-    w_out_counts = lax.all_gather(
-        jnp.concatenate([w_attn_out, beside], axis=1), ("role", "dev"), axis=0, tiled=True
-    )
+    w_qkv_all, w_out_counts = gather(w_qkv, jnp.concatenate([w_attn_out, beside], axis=1))
+    w_qkv_all = w_qkv_all.reshape(-1, w_qkv.shape[1])
+    w_out_counts = w_out_counts.reshape(w_qkv_all.shape[0], -1)
     w_out_all = w_out_counts[:, :model_width]
     counts_all = w_out_counts[:, model_width:].astype(jnp.float32)
     residual = tokens.astype(jnp.float32)

time: 544 us -> 181 us (0.33)
  waiting for transfers between devices: 424 us -> 30.1 us
  Pallas kernels: 0 us -> 39 us
  between operations: 13.6 us -> 0.19 us
  local copies, waits for them, and re-layouts: 4.8 us -> 11.6 us
    all_gather x2 -> x0, waiting for transfers between devices: 393 us -> none  [the longest x1 200 us: shards(): w_qkv_all = lax.all_gather(w_qkv, ('role', 'dev'), axis=0, tiled=True)]
    pallas_call x0 -> x1, Pallas kernels: none -> 39 us  [gather(): pl.pallas_call(gather_kernel, out_shape=[jax.ShapeDtypeStruct(lead + w_qk...]
  transfers between devices with their start and end apart: 3 -> 1, of which waited for: 3 -> 1; matrix products, arithmetic and copies ran while one was open for 1% -> 0% of each run, Pallas kernels for 0% -> 0%
where the time goes in v2:
time: 181 us; the launch traced here: 180 us
  matrix products  46.7 us (26%)
  Pallas kernels  39 us (22%)
  blocking collectives  35.9 us (20%)
  waiting for transfers between devices  30.1 us (17%)
  local copies, waits for them, and re-layouts  11.6 us (6%)
  other arithmetic  11.5 us (6%)
  starting transfers between devices  5.42 us (3%)
    pallas_call x1, Pallas kernels, gather(): pl.pallas_call(gather_kernel, out_shape=[jax.ShapeDtypeStruct(lead + w_qk...  39 us
    all_to_all x1, blocking collectives, shards(): lax.all_to_all(buffer, ('role', 'dev'), split_axis=0, concat_axis=0, tile...  35.9 us
    all_to_all x1, waiting for transfers between devices, shards(): lax.all_to_all(produced.reshape(received.shape), ('role', 'dev'), split_a...  30.1 us
    dot_general x1, matrix products, shards(): jnp.dot(activ, expert_out[0], preferred_element_type=jnp.float32)  17.7 us
    sub x1, matrix products, self_attend(): weights = jnp.exp(scores - row_max)  10.1 us
    dot_general x1, matrix products, self_attend(): jnp.einsum('hst,thd->shd', soft_weights, values, preferred_element_type=j...  7.77 us
    all_to_all x1, starting transfers between devices, shards(): lax.all_to_all(produced.reshape(received.shape), ('role', 'dev'), split_a...  5.42 us
    dot_general x1, matrix products, shards(): jnp.dot(normed, w_qkv_all, preferred_element_type=jnp.float32)  5.11 us
  transfers between devices with their start and end apart: 1, of which 1 were waited for; matrix products, arithmetic and copies ran while one was open for 0% of the time, Pallas kernels for 0%

profile of v2, /device:TPU:1, one launch (start us, length us, event | category | flops | bytes accessed | tf_op | source)
XLA Modules:
  0.0 180.4 jit_solution(10783022327929978639)
XLA Ops:
  0.0 0.0 copy-start
  0.0 0.8 convert_reduce_fusion
  0.8 1.1 fusion.30
  1.9 0.7 convert_element_type.81
  2.6 1.5 fusion.13
  4.1 0.7 pad_maximum_fusion.out_ref
  4.9 0.0 copy-start.1
  4.9 0.8 copy-done.1
  5.7 39.0 %gather_weights.1 = (bf16[2,4,4,2,2,8,3072]{6,5,4,3,2,1,0:T(8,128)(2,1)S(1)}, bf16[2,4,4,2,2,8,1152]{6,5,4,3,2,1,0:T(8,128)(2,1)S(1)}) custom-call(bf16[8,3072]{1,0:T(8,128)(2,1)S(1)} %copy-done.1, bf16[8,1152]{1,0:T(8,128)(2,1)S(1)} %pad_maximum_fusion.out_ref), custom_call_target="tpu_custom_call" | custom-call | tf_op jit(solution)/shard_map/gather_weights/pallas_call | solution.py:118
  44.7 5.1 %convolution_convert_fusion = bf16[512,3072]{1,0:T(8,128)(2,1)S(1)} fusion(bf16[1024,3072]{1,0:T(8,128)(2,1)S(1)} %bitcast.43, bf16[512,1024]{1,0:T(8,128)(2,1)} %param.11, f32[1024]{0:T(1024)S(1)} %convert_element_type.81, f32[512]{0:T(512)S(1)} %add_rsqrt_fusion.1), kind=kOutput, calls=%fused_computation.13 | convolution fusion | flops 3224895488 | bytes 10491904 | tf_op jit(solution)/shard_map/dot_general | solution.py:181
  49.8 1.8 fusion.48
  51.6 2.3 %copy.20 = bf16[512,1024]{0,1:T(8,128)(2,1)} copy(bf16[512,1024]{1,0:T(8,128)(2,1)} %get-tuple-element.11) | data formatting | bytes 2097152 | tf_op jit(solution)/shard_map/slice | solution.py:140
  53.9 0.0 copy-start.5
  53.9 2.3 %copy.21 = bf16[512,1024]{0,1:T(8,128)(2,1)} copy(bf16[512,1024]{1,0:T(8,128)(2,1)} %get-tuple-element.10) | data formatting | bytes 2097152 | tf_op jit(solution)/shard_map/slice | solution.py:138
  56.2 2.3 %copy.22 = bf16[512,1024]{0,1:T(8,128)(2,1)} copy(bf16[512,1024]{1,0:T(8,128)(2,1)} %get-tuple-element.9) | data formatting | bytes 2097152 | tf_op jit(solution)/shard_map/slice | solution.py:139
  58.5 0.0 copy-done.5
  58.5 10.1 %fusion.49 = (f32[16,512]{1,0:T(8,128)S(1)}, f32[16,512,512]{1,2,0:T(8,128)}) fusion(bf16[512,16,64]{0,2,1:T(8,128)(2,1)} %bitcast.47, bf16[512,16,64]{0,2,1:T(8,128)(2,1)} %bitcast.48), kind=kOutput, calls=%fused_computation.73 | convolution fusion | flops 549454336 | bytes 18907136 | tf_op jit(solution)/shard_map/sub | solution.py:145
  68.7 0.0 copy-start.3
  68.7 7.8 %fusion.28 = bf16[16,64,512]{2,1,0:T(8,128)(2,1)S(1)} fusion(bf16[512,16,64]{0,2,1:T(8,128)(2,1)} %bitcast.46, f32[16,512,512]{1,2,0:T(8,128)} %get-tuple-element.15, f32[16,512]{1,0:T(8,128)S(1)} %get-tuple-element.14), kind=kOutput, calls=%fused_computation.28 | convolution fusion | flops 545783808 | bytes 18907136 | tf_op jit(solution)/shard_map/hst,thd->shd/dot_general | solution.py:147
  76.4 0.0 copy-done.3
  76.5 0.0 copy-start.6
  76.5 0.0 copy-start.7
  76.5 0.0 copy-start.4
  76.5 2.6 %multiply_reduce_fusion.1 = (f32[512]{0:T(512)S(1)}, f32[512,1024]{1,0:T(8,128)}) fusion(bf16[512,1024]{0,1:T(8,128)(2,1)S(1)} %bitcast.56, bf16[1024,1152]{1,0:T(8,128)(2,1)S(1)} %bitcast.41, bf16[512,1024]{1,0:T(8,128)(2,1)S(1)} %copy-done.3), kind=kOutput, calls=%fused_computation.27 | convolution fusion | flops 1075838464 | bytes 6293504 | tf_op jit(solution)/shard_map/dot_general | solution.py:183
  79.1 0.0 copy-done.6
  79.1 0.1 compare_reduce_fusion
  79.3 0.2 select_reduce_fusion
  79.5 0.0 copy-done.7
  79.5 0.0 copy-start.2
  79.5 0.2 select_reduce_fusion.2
  79.7 0.0 copy-done.4
  79.7 0.1 select_reduce_fusion.1
  79.8 0.0 copy-done
  79.8 2.3 %fusion.29 = f32[512]{0:T(512)S(1)} fusion(bf16[1024,128]{1,0:T(8,128)(2,1)S(1)} %copy-done, s32[512]{0:T(512)S(1)} %bitcast.52, f32[512,1024]{1,0:T(8,128)} %get-tuple-element.17, f32[1024]{0:T(1024)S(1)} %convert_element_type.93, f32[512]{0:T(512)S(1)} %add_rsqrt_fusion), kind=kOutput, calls=%fused_computation.31 | convolution fusion | flops 135986688 | bytes 2369536 | tf_op jit(solution)/shard_map/dot_general | solution.py:186
  82.2 0.0 copy-done.2
  82.2 4.2 %scatter_custom_fusion = bf16[1024,1024]{1,0:T(8,128)(2,1)} fusion(s32[512]{0:T(512)S(1)} %bitcast.53, bf16[]{:T(256)} %constant.86.clone.1, f32[512,1024]{1,0:T(8,128)S(1)} %copy-done.2, f32[1024]{0:T(1024)S(1)} %convert_element_type.93, f32[512]{0:T(512)S(1)} %add_rsqrt_fusion), kind=kCustom, calls=%fused_computation.33 | custom fusion | flops 1572864 | bytes 4200450 | tf_op jit(solution)/shard_map/scatter | solution.py:214
  86.4 35.9 %all_to_all.10 = bf16[128,8,1024]{2,1,0:T(8,128)(2,1)S(1)} all-to-all(bf16[128,8,1024]{2,1,0:T(8,128)(2,1)} %bitcast.45), channel_id=1, replica_groups=mesh['role'=2,'dev'=64] {'role','dev'}, dimensions={0} | all-to-all | bytes 4194304 | tf_op jit(solution)/shard_map/all_to_all | solution.py:217
  122.3 17.7 %convert_bitcast_fusion = bf16[128,8,1024]{2,1,0:T(8,128)(2,1)} fusion(bf16[1,2816,1024]{2,1,0:T(8,128)(2,1)} %param.19, bf16[1,1024,2816]{2,1,0:T(8,128)(2,1)} %param.18, bf16[128,8,1024]{2,1,0:T(8,128)(2,1)S(1)} %all_to_all.10), kind=kOutput, calls=%fused_computation.25 | convolution fusion | flops 11817975808 | bytes 15728640 | tf_op jit(solution)/shard_map/dot_general | solution.py:222
  139.9 5.4 %all-to-all-start.1 = ((bf16[128,8,1024]{2,1,0:T(8,128)(2,1)}), bf16[128,8,1024]{2,1,0:T(8,128)(2,1)S(1)}, u32[]{:S(2)}, u32[]{:S(2)}) async-start(bf16[128,8,1024]{2,1,0:T(8,128)(2,1)} %convert_bitcast_fusion), calls=%async_computation.1 | async-start | bytes 4194304 | tf_op jit(solution)/shard_map/all_to_all | solution.py:223
  145.4 30.1 %all-to-all-done.1 = bf16[128,8,1024]{2,1,0:T(8,128)(2,1)S(1)} async-done(((bf16[128,8,1024]{2,1,0:T(8,128)(2,1)}), bf16[128,8,1024]{2,1,0:T(8,128)(2,1)S(1)}, u32[]{:S(2)}, u32[]{:S(2)}) %all-to-all-start.1) | async-done | bytes 2097184 | tf_op jit(solution)/shard_map/all_to_all | solution.py:223
  175.5 2.0 %gather_fusion = bf16[512,1024]{1,0:T(8,128)(2,1)S(1)} fusion(bf16[1024,1024]{1,0:T(8,128)(2,1)S(1)} %bitcast.44, s32[1024]{0:T(1024)S(1)} %pad_clamp_fusion), kind=kCustom, calls=%fused_computation | custom fusion | bytes 2099200 | tf_op jit(solution)/shard_map/gather | solution.py:226
  177.6 2.9 %add_convert_fusion = bf16[512,1024]{1,0:T(8,128)(2,1)} fusion(f32[512,1024]{1,0:T(8,128)} %get-tuple-element.17, bf16[512,1024]{1,0:T(8,128)(2,1)S(1)} %gather_fusion, f32[512]{0:T(512)S(1)} %get-tuple-element.12), kind=kLoop, calls=%fused_computation.24 | loop fusion | flops 2097152 | bytes 4196352 | tf_op jit(solution)/shard_map/convert_element_type | solution.py:228
  (11 shorter events, 0.1 us)
Async XLA Ops:
  0.0 79.8 %copy-start = (bf16[1024,128]{1,0:T(8,128)(2,1)S(1)}, bf16[1024,128]{1,0:T(8,128)(2,1)}, u32[]{:S(2)}) copy-start(bf16[1024,128]{1,0:T(8,128)(2,1)} %param.17) | copy-start | bytes 786436
  4.9 0.8 copy-start.1
  53.9 4.6 %copy-start.5 = (bf16[1024]{0:T(1024)(128)(2,1)S(1)}, bf16[1024]{0:T(1024)(128)(2,1)}, u32[]{:S(2)}) copy-start(bf16[1024]{0:T(1024)(128)(2,1)} %param.16) | copy-start | bytes 6148
  68.7 7.8 %copy-start.3 = (bf16[512,1024]{1,0:T(8,128)(2,1)S(1)}, bf16[512,1024]{1,0:T(8,128)(2,1)}, u32[]{:S(2)}) copy-start(bf16[512,1024]{1,0:T(8,128)(2,1)} %param.11) | copy-start | bytes 3145732
  76.5 2.7 %copy-start.6 = (s32[32]{0:T(128)S(1)}, s32[32]{0:T(128)}, u32[]{:S(2)}) copy-start(s32[32]{0:T(128)} %param.21) | copy-start | bytes 388
  76.5 3.0 %copy-start.7 = (s32[128]{0:T(128)S(1)}, s32[128]{0:T(128)}, u32[]{:S(2)}) copy-start(s32[128]{0:T(128)} %param.20) | copy-start | bytes 1540
  76.5 3.2 %copy-start.4 = (s32[512,1]{0,1:T(1,128)S(1)}, s32[512,1]{0,1:T(1,128)}, u32[]{:S(2)}) copy-start(s32[512,1]{0,1:T(1,128)} %param.12) | copy-start | bytes 6148
  79.5 2.7 %copy-start.2 = (f32[512,1024]{1,0:T(8,128)S(1)}, f32[512,1024]{1,0:T(8,128)}, u32[]{:S(2)}) copy-start(f32[512,1024]{1,0:T(8,128)} %get-tuple-element.17) | copy-start | bytes 6291460
  139.9 35.6 %all-to-all-start.1 = ((bf16[128,8,1024]{2,1,0:T(8,128)(2,1)}), bf16[128,8,1024]{2,1,0:T(8,128)(2,1)S(1)}, u32[]{:S(2)}, u32[]{:S(2)}) async-start(bf16[128,8,1024]{2,1,0:T(8,128)(2,1)} %convert_bitcast_fusion), calls=%async_computation.1 | async-start | bytes 4194304 | tf_op jit(solution)/shard_map/all_to_all | solution.py:223

commit v3 on v2

--- a/solution.py
+++ b/solution.py
@@ -124,6 +124,159 @@
         compiler_params=pltpu.CompilerParams(collective_id=0, has_side_effects=True, vmem_limit_bytes=40 << 20),
         name="gather_weights",
     )(w_qkv, w_out)
+
+
+STAGES = 4
+
+
+def shift_of(stage, place):
+    dz, dx, dc = place // 8, place // 2 % 4, place % 2
+    return dz, dx, (stage + 8 - dz - dx) % 4, dc
+
+
+def shifted(at, stage, place, sign):
+    dz, dx, dy, dc = shift_of(stage, place)
+    return {
+        "z": (at["z"] + 4 + sign * dz) % 4,
+        "x": (at["x"] + 4 + sign * dx) % 4,
+        "y": (at["y"] + 4 + sign * dy) % 4,
+        "core": (at["core"] + dc) % 2,
+    }
+
+
+def shift_index(at, expert):
+    dz = (expert // 16 % 4 - at["z"] + 4) % 4
+    dx = (expert // 4 % 4 - at["x"] + 4) % 4
+    dy = (expert // 64 * 2 + expert // 2 % 2 - at["y"] + 4) % 4
+    dc = (expert - at["core"] + 2) % 2
+    return (dz + dx + dy) % 4 * 32 + dz * 8 + dx * 2 + dc
+
+
+def greet_all(me, count):
+    barrier = pltpu.get_barrier_semaphore()
+
+    def greet_one(step, carry):
+        peer = (me + step) % count
+        pl.semaphore_signal(barrier, inc=1, device_id=(peer // 64, peer % 64), device_id_type=MESH)
+        return carry
+
+    lax.fori_loop(1, count, greet_one, 0)
+    return barrier
+
+
+def experts_kernel(
+    normed_ref, hidden_ref, slot_row, slot_col, chosen_col, kept_col, router_ref, w_in_hbm, w_out_hbm, mixed_ref,
+    sent, held, made, back, w_in, w_out, activ, total, weight_sem, send_sem, recv_sem,
+):
+    at = coordinates()
+    me = lax.axis_index("role") * 64 + lax.axis_index("dev")
+    blocks, slot_rows, width = sent.shape
+    per = blocks // STAGES
+    rows = per * slot_rows
+    barrier = greet_all(me, blocks)
+    load_in = pltpu.make_async_copy(w_in_hbm.at[0], w_in, weight_sem.at[0])
+    load_out = pltpu.make_async_copy(w_out_hbm.at[0], w_out, weight_sem.at[1])
+    load_in.start()
+    load_out.start()
+
+    def fill(stage):
+        wanted = lax.broadcasted_iota(jnp.int32, (rows, slot_row.shape[1]), 0) + stage * rows
+        pick = (wanted == slot_row[...]).astype(jnp.bfloat16)
+        block = jnp.dot(pick, normed_ref[...], preferred_element_type=jnp.float32).astype(jnp.bfloat16)
+        sent[pl.ds(stage * per, per)] = block.reshape(per, slot_rows, width)
+
+    def send_out(stage, place, source, target, way):
+        index = stage * per + place
+        pltpu.make_async_remote_copy(
+            src_ref=source.at[index], dst_ref=target.at[index],
+            send_sem=send_sem.at[way], recv_sem=recv_sem.at[way, stage],
+            device_id=device_of(shifted(at, stage, place, 1 - 2 * way)), device_id_type=MESH,
+        ).start()
+
+    def send_stage(stage, source, target, way):
+        first = 1 if stage == 0 else 0
+
+        def one(place, carry):
+            send_out(stage, place, source, target, way)
+            return carry
+
+        lax.fori_loop(first, per, one, 0)
+
+    def stage_arrived(stage, target, way):
+        first = 1 if stage == 0 else 0
+        span = pl.ds(stage * per + first, per - first)
+        pltpu.make_async_copy(target.at[span], target.at[span], recv_sem.at[way, stage]).wait()
+
+    fill(0)
+    pl.semaphore_wait(barrier, blocks - 1)
+    held[0] = sent[0]
+    send_stage(0, sent, held, 0)
+    for stage in range(1, STAGES):
+        fill(stage)
+        send_stage(stage, sent, held, 0)
+    logits = jnp.dot(normed_ref[...], router_ref[...], preferred_element_type=jnp.float32)
+    match = lax.broadcasted_iota(jnp.int32, logits.shape, 1) == chosen_col[...]
+    gate = jax.nn.sigmoid(jnp.sum(jnp.where(match, logits, 0.0), axis=1, keepdims=True)) * kept_col[...]
+    load_in.wait()
+    load_out.wait()
+    total[...] = jnp.zeros_like(total)
+
+    def take_back(stage):
+        stage_arrived(stage, back, 1)
+        if stage == 0:
+            back[0] = made[0]
+        wanted = lax.broadcasted_iota(jnp.int32, (slot_col.shape[0], rows), 1) + stage * rows
+        pick = (wanted == slot_col[...]).astype(jnp.bfloat16)
+        block = back[pl.ds(stage * per, per)].reshape(rows, width)
+        total[...] += jnp.dot(pick, block, preferred_element_type=jnp.float32)
+
+    tile = 256
+    for stage in range(STAGES):
+        stage_arrived(stage, held, 0)
+        block = held[pl.ds(stage * per, per)].reshape(rows, width)
+        for t in range(w_in.shape[1] // tile):
+            span = slice(t * tile, (t + 1) * tile)
+            product = jnp.dot(block, w_in[:, span], preferred_element_type=jnp.float32)
+            activ[:, span] = jnp.maximum(product, 0.0).astype(jnp.bfloat16)
+        for t in range(width // tile):
+            span = slice(t * tile, (t + 1) * tile)
+            product = jnp.dot(activ[...], w_out[:, span], preferred_element_type=jnp.float32)
+            made[pl.ds(stage * per, per), :, span] = product.astype(jnp.bfloat16).reshape(per, slot_rows, tile)
+        send_stage(stage, made, back, 1)
+    for stage in range(STAGES):
+        take_back(stage)
+    mixed_ref[...] = (hidden_ref[...] + gate * total[...]).astype(jnp.bfloat16)
+    for way, source in ((0, sent), (1, made)):
+        span = pl.ds(1, blocks - 1)
+        pltpu.make_async_copy(source.at[span], source.at[span], send_sem.at[way]).wait()
+
+
+def run_experts(normed, hidden, slot, chosen, kept, router, w_in, w_out):
+    tokens, width = normed.shape
+    blocks = router.shape[1]
+    slot_rows = 2 * tokens // blocks
+    exchange = pltpu.VMEM((blocks, slot_rows, width), jnp.bfloat16)
+    vmem = pl.BlockSpec(memory_space=pltpu.VMEM)
+    hbm = pl.BlockSpec(memory_space=pl.ANY)
+    return pl.pallas_call(
+        experts_kernel,
+        out_shape=jax.ShapeDtypeStruct((tokens, width), jnp.bfloat16),
+        in_specs=[vmem] * 7 + [hbm] * 2,
+        out_specs=vmem,
+        scratch_shapes=[
+            exchange, exchange, exchange, exchange,
+            pltpu.VMEM(w_in.shape[1:], jnp.bfloat16),
+            pltpu.VMEM(w_out.shape[1:], jnp.bfloat16),
+            pltpu.VMEM((blocks // STAGES * slot_rows, w_in.shape[2]), jnp.bfloat16),
+            pltpu.VMEM((tokens, width), jnp.float32),
+            pltpu.SemaphoreType.DMA((2,)),
+            pltpu.SemaphoreType.DMA((2,)),
+            pltpu.SemaphoreType.DMA((2, STAGES)),
+        ],
+        compiler_params=pltpu.CompilerParams(collective_id=1, has_side_effects=True, vmem_limit_bytes=56 << 20),
+        cost_estimate=pl.CostEstimate(flops=12 * 10**9, bytes_accessed=20 * 2**20, transcendentals=tokens),
+        name="experts",
+    )(normed, hidden, slot[None, :], slot[:, None], chosen[:, None], kept[:, None], router, w_in, w_out)
 
 
 def rms_scale(values, gain_vector):
@@ -183,8 +336,6 @@
     attended = jnp.dot(context, w_out_all, preferred_element_type=jnp.float32)
     hidden = residual + attended
     normed_ffn = rms_scale(hidden, gain_expert).astype(jnp.bfloat16)
-    logits = jnp.dot(normed_ffn, router, preferred_element_type=jnp.float32)
-    gate = jax.nn.sigmoid(jnp.sum(jnp.where(match, logits, 0.0), axis=1))
     gathered_row = jnp.arange(w_out_counts.shape[0], dtype=jnp.int32)
     first_of_lower = (gathered_row % row_share == 0) & (gathered_row < me * row_share)
     before = jnp.sum(jnp.where(first_of_lower[:, None], counts_all, 0.0), axis=0).astype(jnp.int32)
@@ -205,27 +356,10 @@
         jnp.where(location[:, None] == expert_range[None, :], capacity[None, :], 0), axis=1
     )
     room = jnp.sum(jnp.where(match, (cap_expert - before)[None, :], 0), axis=1)
-    kept = local_rank < room
-    slot_rows = max(2, 2 * seq_len // experts_all)
-    slot_index = chosen * slot_rows + local_rank
-    buffer = (
-        jnp.zeros((experts_all * slot_rows, model_width), jnp.bfloat16)
-        .at[slot_index]
-        .set(normed_ffn)
-    )
-    buffer = buffer.reshape(experts_all, slot_rows, model_width)
-    received = lax.all_to_all(buffer, ("role", "dev"), split_axis=0, concat_axis=0, tiled=True)
-    flat_rows = received.reshape(-1, model_width)
-    activ = jnp.maximum(
-        jnp.dot(flat_rows, expert_in[0], preferred_element_type=jnp.float32), 0.0
-    ).astype(jnp.bfloat16)
-    produced = jnp.dot(activ, expert_out[0], preferred_element_type=jnp.float32).astype(jnp.bfloat16)
-    returned = lax.all_to_all(
-        produced.reshape(received.shape), ("role", "dev"), split_axis=0, concat_axis=0, tiled=True
-    )
-    picked = returned.reshape(-1, model_width)[slot_index].astype(jnp.float32)
-    mixed = hidden + jnp.where(kept, gate, 0.0)[:, None] * picked
-    return mixed.astype(jnp.bfloat16)
+    kept = (local_rank < room).astype(jnp.float32)
+    slot_rows = 2 * seq_len // experts_all
+    slot = shift_index(coordinates(), chosen) * slot_rows + local_rank
+    return run_experts(normed_ffn, hidden, slot, chosen, kept, router, expert_in, expert_out)
 
 
 def solution(mesh):

time: 181 us -> 153 us (0.85); the launches traced: 180 us -> 150 us
  Pallas kernels: 39 us -> 103 us
  blocking collectives: 35.9 us -> 0 us
  waiting for transfers between devices: 30.1 us -> 0 us
  matrix products: 46.7 us -> 24.4 us
  starting transfers between devices: 5.42 us -> 0 us
  other arithmetic: 11.5 us -> 9.1 us
    pallas_call x0 -> x1, Pallas kernels: none -> 64.2 us  [run_experts(): pl.pallas_call(experts_kernel, out_shape=jax.ShapeDtypeStruct((tokens, wi...]
    all_to_all x1 -> x0, blocking collectives: 35.9 us -> none  [shards(): lax.all_to_all(buffer, ('role', 'dev'), split_axis=0, concat_axis=0, tile...]
    all_to_all x1 -> x0, waiting for transfers between devices: 30.1 us -> none  [shards(): lax.all_to_all(produced.reshape(received.shape), ('role', 'dev'), split_a...]
    dot_general x2 -> x0, matrix products: 20 us -> none  [the longest x1 17.7 us: shards(): jnp.dot(activ, expert_out[0], preferred_element_type=jnp.float32)]
    all_to_all x1 -> x0, starting transfers between devices: 5.42 us -> none  [shards(): lax.all_to_all(produced.reshape(received.shape), ('role', 'dev'), split_a...]
    scatter x1 -> x0, other arithmetic: 4.2 us -> none  [shards(): buffer = jnp.zeros((experts_all * slot_rows, model_width), jnp.bfloat16)....]
    unnamed x16 -> x20, local copies, waits for them, and re-layouts: 0.83 us -> 4.53 us
    add x0 -> x2, other arithmetic: none -> 2.8 us  [shards(): slot = shift_index(coordinates(), chosen) * slot_rows + local_rank]
  transfers between devices with their start and end apart: 1 -> 0, of which waited for: 1 -> 0; matrix products, arithmetic and copies ran while one was open for 0% -> 0% of each run, Pallas kernels for 0% -> 0%
where the time goes in v3:
time: 153 us; the launch traced here: 150 us
  Pallas kernels  103 us (67%)
  matrix products  24.4 us (16%)
  local copies, waits for them, and re-layouts  13 us (8%)
  other arithmetic  9.1 us (6%)
    pallas_call x1, Pallas kernels, run_experts(): pl.pallas_call(experts_kernel, out_shape=jax.ShapeDtypeStruct((tokens, wi...  64.2 us
    pallas_call x1, Pallas kernels, gather(): pl.pallas_call(gather_kernel, out_shape=[jax.ShapeDtypeStruct(lead + w_qk...  39 us
    sub x1, matrix products, self_attend(): weights = jnp.exp(scores - row_max)  10.2 us
    dot_general x1, matrix products, self_attend(): jnp.einsum('hst,thd->shd', soft_weights, values, preferred_element_type=j...  7.43 us
    dot_general x1, matrix products, shards(): jnp.dot(normed, w_qkv_all, preferred_element_type=jnp.float32)  5.1 us
    unnamed x20, local copies, waits for them, and re-layouts  4.53 us

profile of v3, /device:TPU:1, one launch (start us, length us, event | category | flops | bytes accessed | tf_op | source)
XLA Modules:
  0.0 150.0 jit_solution(11761226775488745579)
XLA Ops:
  0.0 0.8 convert_reduce_fusion
  0.8 0.7 pad_maximum_fusion.out_ref
  1.5 0.0 copy-start
  1.5 0.8 copy-done
  2.3 39.0 %gather_weights.1 = (bf16[2,4,4,2,2,8,3072]{6,5,4,3,2,1,0:T(8,128)(2,1)S(1)}, bf16[2,4,4,2,2,8,1152]{6,5,4,3,2,1,0:T(8,128)(2,1)S(1)}) custom-call(bf16[8,3072]{1,0:T(8,128)(2,1)S(1)} %copy-done, bf16[8,1152]{1,0:T(8,128)(2,1)S(1)} %pad_maximum_fusion.out_ref), custom_call_target="tpu_custom_call" | custom-call | tf_op jit(solution)/shard_map/gather_weights/pallas_call | solution.py:118
  41.4 0.7 convert_element_type.90
  42.1 1.5 %fusion.8 = f32[512]{0:T(512)S(1)} fusion(bf16[512,1024]{1,0:T(8,128)(2,1)} %param.11), kind=kLoop, calls=%fused_computation.12 | loop fusion | flops 1572352 | bytes 1050624 | tf_op jit(solution)/shard_map/reduce_sum | solution.py:283
  43.6 5.1 %convolution_convert_fusion = bf16[512,3072]{1,0:T(8,128)(2,1)S(1)} fusion(bf16[1024,3072]{1,0:T(8,128)(2,1)S(1)} %bitcast.48, bf16[512,1024]{1,0:T(8,128)(2,1)} %param.11, f32[1024]{0:T(1024)S(1)} %convert_element_type.90, f32[512]{0:T(512)S(1)} %add_rsqrt_fusion.1), kind=kOutput, calls=%fused_computation.7 | convolution fusion | flops 3224895488 | bytes 10491904 | tf_op jit(solution)/shard_map/dot_general | solution.py:334
  48.7 1.6 %fusion.82 = (bf16[512,1024]{1,0:T(8,128)(2,1)S(1)}, bf16[512,1024]{1,0:T(8,128)(2,1)}, bf16[512,1024]{1,0:T(8,128)(2,1)}) fusion(bf16[512,3072]{1,0:T(8,128)(2,1)S(1)} %convolution_convert_fusion), kind=kLoop, calls=%fused_computation.188 | loop fusion | bytes 6291456 | tf_op jit(solution)/shard_map/slice | solution.py:292
  50.3 2.3 %copy.93 = bf16[512,1024]{0,1:T(8,128)(2,1)} copy(bf16[512,1024]{1,0:T(8,128)(2,1)} %get-tuple-element.13) | data formatting | bytes 2097152 | tf_op jit(solution)/shard_map/slice | solution.py:293
  52.6 2.3 %copy.94 = bf16[512,1024]{0,1:T(8,128)(2,1)} copy(bf16[512,1024]{1,0:T(8,128)(2,1)} %get-tuple-element.12) | data formatting | bytes 2097152 | tf_op jit(solution)/shard_map/slice | solution.py:291
  54.9 1.3 copy.95
  56.2 0.0 copy-start.4
  56.3 10.2 %fusion.83 = (f32[16,512]{1,0:T(8,128)S(1)}, f32[16,512,512]{1,2,0:T(8,128)}) fusion(bf16[512,16,64]{0,2,1:T(8,128)(2,1)} %bitcast.50, bf16[512,16,64]{0,2,1:T(8,128)(2,1)} %bitcast.51), kind=kOutput, calls=%fused_computation.189 | convolution fusion | flops 549454336 | bytes 18907136 | tf_op jit(solution)/shard_map/sub | solution.py:298
  66.5 0.0 copy-done.4
  66.5 0.0 copy-start.3
  66.5 7.4 %fusion.15 = bf16[16,64,512]{2,1,0:T(8,128)(2,1)S(1)} fusion(bf16[512,16,64]{0,2,1:T(8,128)(2,1)S(1)} %bitcast.49, f32[16,512,512]{1,2,0:T(8,128)} %get-tuple-element.16, f32[16,512]{1,0:T(8,128)S(1)} %get-tuple-element.15), kind=kOutput, calls=%fused_computation.19 | convolution fusion | flops 545783808 | bytes 18907136 | tf_op jit(solution)/shard_map/hst,thd->shd/dot_general | solution.py:300
  73.9 0.0 copy-done.3
  73.9 0.0 copy-start.6
  73.9 1.4 multiply_reduce_fusion.1
  75.3 0.0 copy-start.1
  75.3 0.0 copy-start.5
  75.3 0.0 copy-start.7
  75.3 0.0 copy-start.8
  75.4 0.0 copy-done.6
  75.4 1.3 copy-done.1
  76.7 1.2 multiply_convert_fusion.normed_ref
  77.9 0.0 copy-done.5
  77.9 0.3 fusion.16
  78.3 0.7 multiply_add_fusion.slot_row
  79.0 0.1 copy.117
  79.1 0.2 copy.116
  79.3 0.1 copy.113
  79.5 0.2 copy.102
  79.7 0.1 copy.97.chosen_col
  79.8 0.0 copy-start.2
  79.8 2.1 %fusion.45.slot_col = s32[512,1]{1,0:T(8,128)} fusion(s32[512,1]{1,0:T(8,128)S(1)} %copy.117, pred[512,1]{1,0:T(8,128)(4,1)S(1)} %copy.116, s32[512,1]{1,0:T(8,128)S(1)} %copy.113, pred[512,1]{1,0:T(8,128)(4,1)S(1)} %copy.102, s32[512,1]{1,0:T(8,128)S(1)} %copy.97.chosen_col, s32[]{:T(128)S(6)} %add.385, s32[]{:T(128)S(6)} %select_n.260, s32[]{:T(128)S(6)} %select_n.255), kind=kLoop, calls=%fused_computation.88 | loop fusion | flops 76288 | bytes 9228 | tf_op jit(solution)/shard_map/add | solution.py:361
  82.0 0.0 copy-done.7
  82.0 0.1 compare_reduce_fusion
  82.1 0.0 copy-done.8
  82.1 0.2 select_reduce_fusion.2
  82.3 0.2 select_reduce_fusion
  82.5 0.1 select_reduce_fusion.1
  82.6 0.2 copy.118
  82.8 0.7 convert_element_type.106.kept_col
  83.6 0.0 copy-done.2
  83.6 64.2 %experts.1 = bf16[512,1024]{1,0:T(8,128)(2,1)} custom-call(bf16[512,1024]{1,0:T(8,128)(2,1)} %multiply_convert_fusion.normed_ref, f32[512,1024]{1,0:T(8,128)} %copy-done.1, s32[1,512]{1,0:T(1,128)} %multiply_add_fusion.slot_row, s32[512,1]{1,0:T(8,128)} %fusion.45.slot_col, s32[512,1]{1,0:T(8,128)} %copy-done.2, f32[512,1]{1,0:T(8,128)} %convert_element_type.106.kept_col, ...), custom_call_target="tpu_custom_call" | custom-call | flops 12000000000 | bytes 20971520 | tf_op jit(solution)/shard_map/experts/pallas_call | solution.py:261
  147.7 2.3 %copy.139 = bf16[512,1024]{1,0:T(8,128)(2,1)} copy(bf16[512,1024]{1,0:T(8,128)(2,1)} %experts.1) | data formatting | bytes 2097152
  (11 shorter events, 0.1 us)
Async XLA Ops:
  1.5 0.8 copy-start
  56.2 10.2 %copy-start.4 = (bf16[512,1024]{0,1:T(8,128)(2,1)S(1)}, bf16[512,1024]{0,1:T(8,128)(2,1)}, u32[]{:S(2)}) copy-start(bf16[512,1024]{0,1:T(8,128)(2,1)} %copy.93) | copy-start | bytes 3145732
  66.5 7.4 %copy-start.3 = (bf16[512,1024]{1,0:T(8,128)(2,1)S(1)}, bf16[512,1024]{1,0:T(8,128)(2,1)}, u32[]{:S(2)}) copy-start(bf16[512,1024]{1,0:T(8,128)(2,1)} %param.11) | copy-start | bytes 3145732
  73.9 1.4 copy-start.6
  75.3 1.4 copy-start.1
  75.3 2.6 %copy-start.5 = (s32[512,1]{0,1:T(1,128)S(1)}, s32[512,1]{0,1:T(1,128)}, u32[]{:S(2)}) copy-start(s32[512,1]{0,1:T(1,128)} %param.12) | copy-start | bytes 6148
  75.3 6.6 %copy-start.7 = (s32[32]{0:T(128)S(1)}, s32[32]{0:T(128)}, u32[]{:S(2)}) copy-start(s32[32]{0:T(128)} %param.21) | copy-start | bytes 388
  75.3 6.7 %copy-start.8 = (s32[128]{0:T(128)S(1)}, s32[128]{0:T(128)}, u32[]{:S(2)}) copy-start(s32[128]{0:T(128)} %param.20) | copy-start | bytes 1540
  79.8 3.7 %copy-start.2 = (s32[512,1]{1,0:T(8,128)}, s32[512,1]{1,0:T(8,128)S(1)}, u32[]{:S(2)}) copy-start(s32[512,1]{1,0:T(8,128)S(1)} %copy.97.chosen_col) | copy-start | bytes 6148

commit v4 on v1

v4 whole, which is shorter than its diff:
```python
import jax
import jax.numpy as jnp
from jax import lax
from jax.experimental import pallas as pl
from jax.experimental.pallas import tpu as pltpu
from jax.sharding import PartitionSpec as P

HEADS = 16
MESH = pl.DeviceIdType.MESH
GROUPS = 4
STAGES = 4
ORDERS = (("z", "x", "y"), ("x", "y", "z"), ("y", "z", "x"))


def coordinates():
    role, dev = lax.axis_index("role"), lax.axis_index("dev")
    return {"z": dev // 16, "x": dev // 4 % 4, "y": role * 2 + dev // 2 % 2, "core": dev % 2}


def device_of(at):
    y = at["y"]
    return (y // 2, ((at["z"] * 4 + at["x"]) * 2 + y % 2) * 2 + at["core"])


def moved(at, axis, by):
    size = 2 if axis == "core" else 4
    return {**at, axis: (at[axis] + by) % size}


def block_of(buf, at, whole, cols):
    every = slice(None)
    yh, yl = (every, every) if "y" in whole else (at["y"] // 2, at["y"] % 2)
    z = every if "z" in whole else at["z"]
    x = every if "x" in whole else at["x"]
    return buf.at[yh, z, x, yl, at["core"], every, slice(*cols)]


def shift_of(stage, place):
    dz, dx, dc = place // 8, place // 2 % 4, place % 2
    return dz, dx, (stage + 8 - dz - dx) % 4, dc


def shifted(at, stage, place, sign):
    dz, dx, dy, dc = shift_of(stage, place)
    return {
        "z": (at["z"] + 4 + sign * dz) % 4,
        "x": (at["x"] + 4 + sign * dx) % 4,
        "y": (at["y"] + 4 + sign * dy) % 4,
        "core": (at["core"] + dc) % 2,
    }


def shift_index(at, expert):
    dz = ((expert >> 4) - at["z"] + 4) & 3
    dx = ((expert >> 2) - at["x"] + 4) & 3
    dy = ((expert >> 6) * 2 + ((expert >> 1) & 1) - at["y"] + 4) & 3
    dc = (expert - at["core"] + 2) & 1
    return ((dz + dx + dy) & 3) * 32 + dz * 8 + dx * 2 + dc


class Piece:
    def __init__(self, buf, cols, order, at, send, recv, first):
        self.buf, self.cols, self.order, self.at = buf, cols, order, at
        self.send, self.recv, self.first = send, recv, first
        self.started = []

    def copy(self, block_at, whole, to, slot):
        ref = block_of(self.buf, block_at, whole, self.cols)
        return pltpu.make_async_remote_copy(
            src_ref=ref,
            dst_ref=ref,
            send_sem=self.send.at[self.first + slot],
            recv_sem=self.recv.at[self.first + slot],
            device_id=device_of(to),
            device_id_type=MESH,
        )

    def start(self, *args):
        copy = self.copy(*args)
        copy.start()
        self.started.append(copy)

    def open(self, phase):
        axis, whole = self.order[phase], self.order[:phase]
        for by in (1, 3, 2):
            self.start(self.at, whole, moved(self.at, axis, by), phase * 3 + by - 1)

    def arrive(self, phase):
        axis, whole = self.order[phase], self.order[:phase]
        for by in (1, 3, 2):
            source = moved(self.at, axis, -by % 4)
            self.copy(source, whole, source, phase * 3 + by - 1).wait_recv()

    def hand_over(self):
        self.start(self.at, self.order, moved(self.at, "core", 1), 9)

    def taken_over(self):
        other = moved(self.at, "core", 1)
        self.copy(other, self.order, other, 9).wait_recv()

    def drain(self):
        for copy in self.started:
            copy.wait_send()


def greet(at):
    barrier = pltpu.get_barrier_semaphore()
    near = [(axis, by) for axis in ("z", "x", "y") for by in (1, 2, 3)] + [("core", 1)]
    for axis, by in near:
        pl.semaphore_signal(
            barrier, inc=1, device_id=device_of(moved(at, axis, by)), device_id_type=MESH
        )
    return barrier, len(near)


def rms_scale(values, gain):
    mean_sq = jnp.mean(values * values, axis=-1, keepdims=True)
    return values * lax.rsqrt(mean_sq + 1e-06) * gain


def layer_kernel(
    swap_ref, tokens_ref, chosen_ref, qkv_ref, out_ref, gains_ref, router_ref,
    capacity_ref, w_in_hbm, w_out_hbm, mixed_ref,
    qkv_all, out_all, normed, queries, keys, values, summed, context, hidden,
    sent, held, made, back, w_in, w_out, activ, total,
    weight_sem, gather_send, gather_recv, send_sem, recv_sem,
):
    at = coordinates()
    me = lax.axis_index("role") * 64 + lax.axis_index("dev")
    seq_len, width = tokens_ref.shape
    experts_all = router_ref.shape[1]
    barrier, greeted = greet(at)
    load_in = pltpu.make_async_copy(w_in_hbm.at[0], w_in, weight_sem.at[0])
    load_out = pltpu.make_async_copy(w_out_hbm.at[0], w_out, weight_sem.at[1])
    load_in.start()
    load_out.start()

    own = (at["y"] // 2, at["z"], at["x"], at["y"] % 2, at["core"])
    chosen = chosen_ref[...]
    match_t = (
        lax.broadcasted_iota(jnp.int32, (experts_all, seq_len), 0) == chosen
    ).astype(jnp.float32)
    match = match_t.T
    match_low = match.astype(jnp.bfloat16)
    qkv_all[own] = qkv_ref[...]
    share = out_ref.shape[0]
    counts = jnp.dot(
        jnp.ones((share, seq_len), jnp.bfloat16), match_low, preferred_element_type=jnp.float32
    )
    out_all[own] = jnp.concatenate([out_ref[...], counts.astype(jnp.bfloat16)], axis=1)

    chunks, made_pieces = [], 0
    heads_wide = width // GROUPS
    beside = width + experts_all
    spans = [(qkv_all, g * heads_wide, heads_wide, width) for g in range(GROUPS)]
    spans.append((out_all, 0, beside // 3, beside // 3))
    for buf, first, wide, stride in spans:
        chunk = []
        for n, order in enumerate(ORDERS):
            cols = (first + n * stride, first + n * stride + wide)
            chunk.append(Piece(buf, cols, order, at, gather_send, gather_recv, 10 * made_pieces))
            made_pieces += 1
        chunks.append(chunk)

    pl.semaphore_wait(barrier, greeted)
    for chunk in chunks:
        for piece in chunk:
            piece.open(0)
    normed[...] = rms_scale(tokens_ref[...].astype(jnp.float32), gains_ref[0:1]).astype(
        jnp.bfloat16
    )
    for phase in (0, 1):
        for chunk in chunks:
            for piece in chunk:
                piece.arrive(phase)
                piece.open(phase + 1)

    row_ids = lax.broadcasted_iota(jnp.int32, (seq_len, seq_len), 0)
    col_ids = lax.broadcasted_iota(jnp.int32, (seq_len, seq_len), 1)
    lower = (col_ids < row_ids).astype(jnp.bfloat16)
    upper = (row_ids < col_ids).astype(jnp.bfloat16)
    rank_t = jnp.dot(match_t.astype(jnp.bfloat16), upper, preferred_element_type=jnp.float32)
    rank = jnp.dot(lower, match_low, preferred_element_type=jnp.float32)
    rank_col = jnp.sum(match * rank, axis=1, keepdims=True)
    slot_rows = sent.shape[1]
    first_t = shift_index(
        at, lax.broadcasted_iota(jnp.int32, (experts_all, seq_len), 0)
    ).astype(jnp.float32) * slot_rows
    first_row = shift_index(
        at, lax.broadcasted_iota(jnp.int32, (1, experts_all), 1)
    ).astype(jnp.float32) * slot_rows
    slot_row = jnp.sum(match_t * (rank_t + first_t), axis=0, keepdims=True).astype(jnp.int32)
    slot_col = jnp.sum(match * (rank + first_row), axis=1, keepdims=True).astype(jnp.int32)

    def hand_over(chunk):
        for piece in chunk:
            piece.arrive(2)
            piece.hand_over()

    def head_step(head, carry):
        lane = lax.broadcasted_iota(jnp.int32, (1, heads_wide), 1)
        size = width // HEADS
        here = jnp.where((lane // size) == head, 1.0, 0.0).astype(jnp.bfloat16)
        value = values[...] * here
        for half in range(2):
            rows = slice(half * seq_len // 2, (half + 1) * seq_len // 2)
            scores = lax.dot_general(
                queries[rows, :] * here, keys[...], (((1,), (1,)), ((), ())),
                preferred_element_type=jnp.float32,
            )
            weights = jnp.exp(scores - jnp.max(scores, axis=1, keepdims=True))
            norm = 1.0 / jnp.sum(weights, axis=1, keepdims=True)
            part = jnp.dot(weights.astype(jnp.bfloat16), value, preferred_element_type=jnp.float32)
            summed[rows, :] += part * norm
        return carry

    hand_over(chunks[0])
    per_group = HEADS // GROUPS
    scale = (width // HEADS) ** -0.5
    for g in range(GROUPS):
        for piece in chunks[g]:
            piece.taken_over()
        for n, target in enumerate((queries, keys, values)):
            first = n * width + g * heads_wide
            weight = qkv_all[:, :, :, :, :, :, first : first + heads_wide].reshape(width, heads_wide)
            product = jnp.dot(normed[...], weight, preferred_element_type=jnp.float32)
            product = product.astype(jnp.bfloat16)
            target[...] = product * jnp.bfloat16(scale) if n == 0 else product
        summed[...] = jnp.zeros_like(summed)
        lax.fori_loop(0, per_group // 2, head_step, 0)
        hand_over(chunks[g + 1])
        lax.fori_loop(per_group // 2, per_group, head_step, 0)
        context[:, g * heads_wide : (g + 1) * heads_wide] = summed[...].astype(jnp.bfloat16)

    for piece in chunks[GROUPS]:
        piece.taken_over()
    for g in range(GROUPS):
        span = slice(g * heads_wide, (g + 1) * heads_wide)
        weight = out_all[:, :, :, :, :, :, span].reshape(width, heads_wide)
        product = jnp.dot(context[...], weight, preferred_element_type=jnp.float32)
        hidden[:, span] = tokens_ref[:, span].astype(jnp.float32) + product
    normed[...] = rms_scale(hidden[...], gains_ref[1:2]).astype(jnp.bfloat16)

    blocks = sent.shape[0]
    per = blocks // STAGES
    rows = per * slot_rows

    def fill(stage):
        wanted = lax.broadcasted_iota(jnp.int32, (rows, seq_len), 0) + stage * rows
        pick = (wanted == slot_row).astype(jnp.bfloat16)
        block = jnp.dot(pick, normed[...], preferred_element_type=jnp.float32).astype(jnp.bfloat16)
        sent[pl.ds(stage * per, per)] = block.reshape(per, slot_rows, width)

    def send_stage(stage, source, target, way):
        def one(place, carry):
            index = stage * per + place
            pltpu.make_async_remote_copy(
                src_ref=source.at[index],
                dst_ref=target.at[index],
                send_sem=send_sem.at[way],
                recv_sem=recv_sem.at[way, stage],
                device_id=device_of(shifted(at, stage, place, 1 - 2 * way)),
                device_id_type=MESH,
            ).start()
            return carry

        lax.fori_loop(1 if stage == 0 else 0, per, one, 0)

    def stage_arrived(stage, target, way):
        first = 1 if stage == 0 else 0
        span = pl.ds(stage * per + first, per - first)
        pltpu.make_async_copy(target.at[span], target.at[span], recv_sem.at[way, stage]).wait()

    for stage in range(STAGES):
        fill(stage)
        if stage == 0:
            held[0] = sent[0]
        send_stage(stage, sent, held, 0)

    counts_all = out_all[:, :, :, :, :, :, width:beside].reshape(width, experts_all)
    row_of = lax.broadcasted_iota(jnp.int32, (8, width), 1)
    lower_rows = ((row_of % share == 0) & (row_of < me * share)).astype(jnp.bfloat16)
    before = jnp.dot(lower_rows, counts_all, preferred_element_type=jnp.float32)[0:1]
    dev_of = lax.broadcasted_iota(jnp.int32, (1, experts_all), 1) % (experts_all // 2)
    flagged = jnp.zeros((1, experts_all), jnp.int32)
    for n in range(swap_ref.shape[0]):
        flagged = jnp.maximum(flagged, (dev_of == swap_ref[n]).astype(jnp.int32))
    capacity = capacity_ref[...]
    half = experts_all // 2
    traded = jnp.concatenate([capacity[:, half:], capacity[:, :half]], axis=1)
    room = jnp.where(flagged > 0, traded, capacity).astype(jnp.float32) - before
    kept = rank_col < jnp.sum(match * room, axis=1, keepdims=True)
    logits = jnp.dot(normed[...], router_ref[...], preferred_element_type=jnp.float32)
    gate = jax.nn.sigmoid(jnp.sum(match * logits, axis=1, keepdims=True))
    gate = jnp.where(kept, gate, 0.0)
    load_in.wait()
    load_out.wait()
    total[...] = jnp.zeros_like(total)

    tile = 256
    for stage in range(STAGES):
        stage_arrived(stage, held, 0)
        block = held[pl.ds(stage * per, per)].reshape(rows, width)
        for t in range(w_in.shape[1] // tile):
            span = slice(t * tile, (t + 1) * tile)
            product = jnp.dot(block, w_in[:, span], preferred_element_type=jnp.float32)
            activ[:, span] = jnp.maximum(product, 0.0).astype(jnp.bfloat16)
        for t in range(width // tile):
            span = slice(t * tile, (t + 1) * tile)
            product = jnp.dot(activ[...], w_out[:, span], preferred_element_type=jnp.float32)
            made[pl.ds(stage * per, per), :, span] = product.astype(jnp.bfloat16).reshape(
                per, slot_rows, tile
            )
        send_stage(stage, made, back, 1)
    for stage in range(STAGES):
        stage_arrived(stage, back, 1)
        if stage == 0:
            back[0] = made[0]
        wanted = lax.broadcasted_iota(jnp.int32, (seq_len, rows), 1) + stage * rows
        pick = (wanted == slot_col).astype(jnp.bfloat16)
        block = back[pl.ds(stage * per, per)].reshape(rows, width)
        total[...] += jnp.dot(pick, block, preferred_element_type=jnp.float32)
    mixed_ref[...] = (hidden[...] + gate * total[...]).astype(jnp.bfloat16)
    for way, source in ((0, sent), (1, made)):
        span = pl.ds(1, blocks - 1)
        pltpu.make_async_copy(source.at[span], source.at[span], send_sem.at[way]).wait()
    for chunk in chunks:
        for piece in chunk:
            piece.drain()


def shards(
    tokens,
    expert_ids,
    w_qkv,
    w_attn_out,
    gain_attn,
    gain_expert,
    router,
    expert_in,
    expert_out,
    capacity,
    swap_list,
):
    seq_len, width = tokens.shape
    experts_all = router.shape[1]
    slot_rows = 2 * seq_len // experts_all
    lead = (2, 4, 4, 2, 2)
    low, wide = jnp.bfloat16, width // GROUPS
    exchange = pltpu.VMEM((experts_all, slot_rows, width), low)
    vmem = pl.BlockSpec(memory_space=pltpu.VMEM)
    hbm = pl.BlockSpec(memory_space=pl.ANY)
    copies = 10 * 3 * (GROUPS + 1)
    return pl.pallas_call(
        layer_kernel,
        out_shape=jax.ShapeDtypeStruct((seq_len, width), low),
        in_specs=[pl.BlockSpec(memory_space=pltpu.SMEM)] + [vmem] * 7 + [hbm] * 2,
        out_specs=vmem,
        scratch_shapes=[
            pltpu.VMEM(lead + w_qkv.shape, low),
            pltpu.VMEM(lead + (w_attn_out.shape[0], width + experts_all), low),
            pltpu.VMEM((seq_len, width), low),
            pltpu.VMEM((seq_len, wide), low),
            pltpu.VMEM((seq_len, wide), low),
            pltpu.VMEM((seq_len, wide), low),
            pltpu.VMEM((seq_len, wide), jnp.float32),
            pltpu.VMEM((seq_len, width), low),
            pltpu.VMEM((seq_len, width), jnp.float32),
            exchange,
            exchange,
            exchange,
            exchange,
            pltpu.VMEM(expert_in.shape[1:], low),
            pltpu.VMEM(expert_out.shape[1:], low),
            pltpu.VMEM((experts_all // STAGES * slot_rows, expert_in.shape[2]), low),
            pltpu.VMEM((seq_len, width), jnp.float32),
            pltpu.SemaphoreType.DMA((2,)),
            pltpu.SemaphoreType.DMA((copies,)),
            pltpu.SemaphoreType.DMA((copies,)),
            pltpu.SemaphoreType.DMA((2,)),
            pltpu.SemaphoreType.DMA((2, STAGES)),
        ],
        compiler_params=pltpu.CompilerParams(
            collective_id=0, has_side_effects=True, vmem_limit_bytes=58 << 20
        ),
        name="encoder_layer",
    )(
        swap_list, tokens, expert_ids.reshape(1, seq_len), w_qkv, w_attn_out,
        jnp.stack([gain_attn, gain_expert]).astype(jnp.float32), router, capacity[None, :], expert_in, expert_out,
    )


def solution(mesh):
    return jax.shard_map(
        shards,
        mesh=mesh,
        in_specs=(
            P(("role", "dev"), None),
            P(("role", "dev"), None),
            P(("role", "dev"), None),
            P(("role", "dev"), None),
            P(),
            P(),
            P(),
            P(("role", "dev"), None, None),
            P(("role", "dev"), None, None),
            P(),
            P(),
        ),
        out_specs=P(("role", "dev"), None),
        check_vma=False,
    )
```

time: 544 us -> 118 us (0.22)
  waiting for transfers between devices: 424 us -> 0 us
  Pallas kernels: 0 us -> 114 us
  matrix products: 43.8 us -> 0 us
  blocking collectives: 37.2 us -> 0 us
  other arithmetic: 15.1 us -> 0.61 us
  between operations: 13.6 us -> 0.01 us
  starting transfers between devices: 5.47 us -> 0 us
    all_gather x2 -> x0, waiting for transfers between devices: 393 us -> none  [the longest x1 200 us: shards(): w_qkv_all = lax.all_gather(w_qkv, ('role', 'dev'), axis=0, tiled=True)]
    pallas_call x0 -> x1, Pallas kernels: none -> 114 us  [shards(): pl.pallas_call(layer_kernel, out_shape=jax.ShapeDtypeStruct((seq_len, wid...]
    all_to_all x1 -> x0, blocking collectives: 37.2 us -> none  [shards(): lax.all_to_all(buffer, ('role', 'dev'), split_axis=0, concat_axis=0, tile...]
    dot_general x6 -> x0, matrix products: 34.9 us -> none  [the longest x1 17.7 us: shards(): jnp.dot(activ, expert_out[0], preferred_element_type=jnp.float32)]
    all_to_all x1 -> x0, waiting for transfers between devices: 30.1 us -> none  [shards(): lax.all_to_all(produced.reshape(received.shape), ('role', 'dev'), split_a...]
    sub x1 -> x0, matrix products: 8.93 us -> none  [self_attend(): weights = jnp.exp(scores - row_max)]
  transfers between devices with their start and end apart: 3 -> 0, of which waited for: 3 -> 0; matrix products, arithmetic and copies ran while one was open for 1% -> 0% of each run, Pallas kernels for 0% -> 0%
where the time goes in v4:
time: 118 us
  Pallas kernels  114 us (97%)
  local copies, waits for them, and re-layouts  3.63 us (3%)
    pallas_call x1, Pallas kernels, shards(): pl.pallas_call(layer_kernel, out_shape=jax.ShapeDtypeStruct((seq_len, wid...  114 us

profile of v4, /device:TPU:1, one launch (start us, length us, event | category | flops | bytes accessed | tf_op | source)
XLA Modules:
  0.0 118.0 jit_solution(923261359134644300)
XLA Ops:
  0.0 0.7 stack.9
  0.7 0.7 stack.10
  1.4 0.6 maximum_convert_fusion.gains_ref
  2.0 113.8 %encoder_layer.1 = bf16[512,1024]{1,0:T(8,128)(2,1)} custom-call(s32[32]{0:T(128)} %swap_ref.1, bf16[512,1024]{1,0:T(8,128)(2,1)} %tokens_ref.1, s32[1,512]{1,0:T(1,128)} %bitcast.2, bf16[8,3072]{1,0:T(8,128)(2,1)} %qkv_ref.1, bf16[8,1024]{1,0:T(8,128)(2,1)} %out_ref.1, f32[2,1024]{1,0:T(2,128)} %maximum_convert_fusion.gains_ref, ...), custom_call_target="tpu_custom_call" | custom-call | tf_op jit(solution)/shard_map/encoder_layer/pallas_call | solution.py:354
  115.8 2.3 %copy.13 = bf16[512,1024]{1,0:T(8,128)(2,1)} copy(bf16[512,1024]{1,0:T(8,128)(2,1)} %encoder_layer.1) | data formatting | bytes 2097152

commit v5 on v4

--- a/solution.py
+++ b/solution.py
@@ -35,15 +35,19 @@
     return buf.at[yh, z, x, yl, at["core"], every, slice(*cols)]
 
 
-def shift_of(stage, place):
-    dz, dx, dc = place // 8, place // 2 % 4, place % 2
-    return dz, dx, (stage + 8 - dz - dx) % 4, dc
-
-
-def shifted(at, stage, place, sign):
-    dz, dx, dy, dc = shift_of(stage, place)
+TWICE = (0, 2, 3, 1)
+THRICE = (0, 3, 1, 2)
+
+
+def crossed(two_bits, mask):
+    return (two_bits, two_bits + 1 - 2 * (two_bits % 2), (two_bits + 2) % 4, 3 - two_bits)[mask]
+
+
+def shifted(at, stage, turn, step, dc, sign):
+    dx = crossed(turn, TWICE[step])
+    dy = crossed(stage, THRICE[step])
     return {
-        "z": (at["z"] + 4 + sign * dz) % 4,
+        "z": (at["z"] + 4 + sign * step) % 4,
         "x": (at["x"] + 4 + sign * dx) % 4,
         "y": (at["y"] + 4 + sign * dy) % 4,
         "core": (at["core"] + dc) % 2,
@@ -55,7 +59,9 @@
     dx = ((expert >> 2) - at["x"] + 4) & 3
     dy = ((expert >> 6) * 2 + ((expert >> 1) & 1) - at["y"] + 4) & 3
     dc = (expert - at["core"] + 2) & 1
-    return ((dz + dx + dy) & 3) * 32 + dz * 8 + dx * 2 + dc
+    twice = ((dz >> 1) ^ (dz & 1)) * 2 + (dz >> 1)
+    turn, stage = dx ^ twice, dy ^ twice ^ dz
+    return stage * 32 + turn * 8 + dz * 2 + dc
 
 
 class Piece:
@@ -252,19 +258,27 @@
         sent[pl.ds(stage * per, per)] = block.reshape(per, slot_rows, width)
 
     def send_stage(stage, source, target, way):
-        def one(place, carry):
-            index = stage * per + place
+        def send_block(turn, step, dc):
+            index = stage * per + turn * 8 + step * 2 + dc
             pltpu.make_async_remote_copy(
                 src_ref=source.at[index],
                 dst_ref=target.at[index],
                 send_sem=send_sem.at[way],
                 recv_sem=recv_sem.at[way, stage],
-                device_id=device_of(shifted(at, stage, place, 1 - 2 * way)),
+                device_id=device_of(shifted(at, stage, turn, step, dc, 1 - 2 * way)),
                 device_id_type=MESH,
             ).start()
+
+        def send_turn(turn, carry):
+            for step in range(4):
+                for dc in range(2):
+                    if stage == 0 and step == 0 and dc == 0:
+                        pl.when(turn > 0)(lambda: send_block(turn, 0, 0))
+                    else:
+                        send_block(turn, step, dc)
             return carry
 
-        lax.fori_loop(1 if stage == 0 else 0, per, one, 0)
+        lax.fori_loop(0, 4, send_turn, 0)
 
     def stage_arrived(stage, target, way):
         first = 1 if stage == 0 else 0

time: 118 us -> 105 us (0.89)
  Pallas kernels: 114 us -> 100 us
    pallas_call x1, Pallas kernels: 114 us -> 100 us  [shards(): pl.pallas_call(layer_kernel, out_shape=jax.ShapeDtypeStruct((seq_len, wid...]
where the time goes in v5:
time: 105 us; the launch traced here: 104 us
  Pallas kernels  100 us (95%)
  local copies, waits for them, and re-layouts  3.63 us (3%)
    pallas_call x1, Pallas kernels, shards(): pl.pallas_call(layer_kernel, out_shape=jax.ShapeDtypeStruct((seq_len, wid...  100 us
    unnamed x1, local copies, waits for them, and re-layouts  2.26 us

profile of v5, /device:TPU:1, one launch (start us, length us, event | category | flops | bytes accessed | tf_op | source)
XLA Modules:
  0.0 104.5 jit_solution(5946260516512734810)
XLA Ops:
  0.0 0.7 stack.9
  0.7 0.7 stack.10
  1.4 0.6 maximum_convert_fusion.gains_ref
  2.0 100.2 %encoder_layer.1 = bf16[512,1024]{1,0:T(8,128)(2,1)} custom-call(s32[32]{0:T(128)} %swap_ref.1, bf16[512,1024]{1,0:T(8,128)(2,1)} %tokens_ref.1, s32[1,512]{1,0:T(1,128)} %bitcast.2, bf16[8,3072]{1,0:T(8,128)(2,1)} %qkv_ref.1, bf16[8,1024]{1,0:T(8,128)(2,1)} %out_ref.1, f32[2,1024]{1,0:T(2,128)} %maximum_convert_fusion.gains_ref, ...), custom_call_target="tpu_custom_call" | custom-call | tf_op jit(solution)/shard_map/encoder_layer/pallas_call | solution.py:368
  102.2 2.3 %copy.13 = bf16[512,1024]{1,0:T(8,128)(2,1)} copy(bf16[512,1024]{1,0:T(8,128)(2,1)} %encoder_layer.1) | data formatting | bytes 2097152

commit v6 on v5

--- a/solution.py
+++ b/solution.py
@@ -121,13 +121,13 @@
 
 def rms_scale(values, gain):
     mean_sq = jnp.mean(values * values, axis=-1, keepdims=True)
-    return values * lax.rsqrt(mean_sq + 1e-06) * gain
+    return values * lax.rsqrt(mean_sq + 1e-06) * gain.astype(jnp.float32).reshape(1, -1)
 
 
 def layer_kernel(
-    swap_ref, tokens_ref, chosen_ref, qkv_ref, out_ref, gains_ref, router_ref,
+    swap_ref, tokens_hbm, chosen_ref, qkv_ref, out_ref, gain_attn_ref, gain_expert_ref, router_hbm,
     capacity_ref, w_in_hbm, w_out_hbm, mixed_ref,
-    qkv_all, out_all, normed, queries, keys, values, summed, context, hidden,
+    tokens_ref, router_ref, qkv_all, out_all, normed, queries, keys, values, summed, context, hidden,
     sent, held, made, back, w_in, w_out, activ, total,
     weight_sem, gather_send, gather_recv, send_sem, recv_sem,
 ):
@@ -138,6 +138,10 @@
     barrier, greeted = greet(at)
     load_in = pltpu.make_async_copy(w_in_hbm.at[0], w_in, weight_sem.at[0])
     load_out = pltpu.make_async_copy(w_out_hbm.at[0], w_out, weight_sem.at[1])
+    load_tokens = pltpu.make_async_copy(tokens_hbm, tokens_ref, weight_sem.at[2])
+    load_router = pltpu.make_async_copy(router_hbm, router_ref, weight_sem.at[3])
+    load_tokens.start()
+    load_router.start()
     load_in.start()
     load_out.start()
 
@@ -172,7 +176,8 @@
     for chunk in chunks:
         for piece in chunk:
             piece.open(0)
-    normed[...] = rms_scale(tokens_ref[...].astype(jnp.float32), gains_ref[0:1]).astype(
+    load_tokens.wait()
+    normed[...] = rms_scale(tokens_ref[...].astype(jnp.float32), gain_attn_ref[...]).astype(
         jnp.bfloat16
     )
     for phase in (0, 1):
@@ -233,9 +238,8 @@
             product = product.astype(jnp.bfloat16)
             target[...] = product * jnp.bfloat16(scale) if n == 0 else product
         summed[...] = jnp.zeros_like(summed)
-        lax.fori_loop(0, per_group // 2, head_step, 0)
         hand_over(chunks[g + 1])
-        lax.fori_loop(per_group // 2, per_group, head_step, 0)
+        lax.fori_loop(0, per_group, head_step, 0)
         context[:, g * heads_wide : (g + 1) * heads_wide] = summed[...].astype(jnp.bfloat16)
 
     for piece in chunks[GROUPS]:
@@ -245,7 +249,7 @@
         weight = out_all[:, :, :, :, :, :, span].reshape(width, heads_wide)
         product = jnp.dot(context[...], weight, preferred_element_type=jnp.float32)
         hidden[:, span] = tokens_ref[:, span].astype(jnp.float32) + product
-    normed[...] = rms_scale(hidden[...], gains_ref[1:2]).astype(jnp.bfloat16)
+    normed[...] = rms_scale(hidden[...], gain_expert_ref[...]).astype(jnp.bfloat16)
 
     blocks = sent.shape[0]
     per = blocks // STAGES
@@ -304,6 +308,7 @@
     traded = jnp.concatenate([capacity[:, half:], capacity[:, :half]], axis=1)
     room = jnp.where(flagged > 0, traded, capacity).astype(jnp.float32) - before
     kept = rank_col < jnp.sum(match * room, axis=1, keepdims=True)
+    load_router.wait()
     logits = jnp.dot(normed[...], router_ref[...], preferred_element_type=jnp.float32)
     gate = jax.nn.sigmoid(jnp.sum(match * logits, axis=1, keepdims=True))
     gate = jnp.where(kept, gate, 0.0)
@@ -368,9 +373,11 @@
     return pl.pallas_call(
         layer_kernel,
         out_shape=jax.ShapeDtypeStruct((seq_len, width), low),
-        in_specs=[pl.BlockSpec(memory_space=pltpu.SMEM)] + [vmem] * 7 + [hbm] * 2,
+        in_specs=[pl.BlockSpec(memory_space=pltpu.SMEM), hbm] + [vmem] * 5 + [hbm, vmem] + [hbm] * 2,
         out_specs=vmem,
         scratch_shapes=[
+            pltpu.VMEM(tokens.shape, low),
+            pltpu.VMEM(router.shape, low),
             pltpu.VMEM(lead + w_qkv.shape, low),
             pltpu.VMEM(lead + (w_attn_out.shape[0], width + experts_all), low),
             pltpu.VMEM((seq_len, width), low),
@@ -388,7 +395,7 @@
             pltpu.VMEM(expert_out.shape[1:], low),
             pltpu.VMEM((experts_all // STAGES * slot_rows, expert_in.shape[2]), low),
             pltpu.VMEM((seq_len, width), jnp.float32),
-            pltpu.SemaphoreType.DMA((2,)),
+            pltpu.SemaphoreType.DMA((4,)),
             pltpu.SemaphoreType.DMA((copies,)),
             pltpu.SemaphoreType.DMA((copies,)),
             pltpu.SemaphoreType.DMA((2,)),
@@ -400,7 +407,7 @@
         name="encoder_layer",
     )(
         swap_list, tokens, expert_ids.reshape(1, seq_len), w_qkv, w_attn_out,
-        jnp.stack([gain_attn, gain_expert]).astype(jnp.float32), router, capacity[None, :], expert_in, expert_out,
+        gain_attn, gain_expert, router, capacity[None, :], expert_in, expert_out,
     )
 
 

time: 105 us -> 98.8 us (0.941)
  Pallas kernels: 100 us -> 96.3 us
  local copies, waits for them, and re-layouts: 3.63 us -> 2.26 us
    pallas_call x1, Pallas kernels: 100 us -> 96.3 us  [shards(): pl.pallas_call(layer_kernel, out_shape=jax.ShapeDtypeStruct((seq_len, wid...]
    another operation x2 -> x0, local copies, waits for them, and re-layouts: 1.37 us -> none  [shards(): jnp.stack([gain_attn, gain_expert]).astype(jnp.float32)]
where the time goes in v6:
time: 98.8 us; the launch traced here: 98.6 us
  Pallas kernels  96.3 us (97%)
  local copies, waits for them, and re-layouts  2.26 us (2%)
    pallas_call x1, Pallas kernels, shards(): pl.pallas_call(layer_kernel, out_shape=jax.ShapeDtypeStruct((seq_len, wid...  96.3 us
    unnamed x1, local copies, waits for them, and re-layouts  2.26 us

profile of v6, /device:TPU:1, one launch (start us, length us, event | category | flops | bytes accessed | tf_op | source)
XLA Modules:
  0.0 98.6 jit_solution(3824691476724861538)
XLA Ops:
  0.0 96.3 %encoder_layer.1 = bf16[512,1024]{1,0:T(8,128)(2,1)} custom-call(s32[32]{0:T(128)} %swap_ref.1, bf16[512,1024]{1,0:T(8,128)(2,1)} %tokens_hbm.1, s32[1,512]{1,0:T(1,128)} %bitcast.2, bf16[8,3072]{1,0:T(8,128)(2,1)} %qkv_ref.1, bf16[8,1024]{1,0:T(8,128)(2,1)} %out_ref.1, bf16[1024]{0:T(1024)(128)(2,1)} %gain_attn_ref.1, bf16[1024]{0:T(1024)(128)(2,1)} %gain_expert_ref.1, ...), custom_call_target="tpu_custom_call" | custom-call | tf_op jit(solution)/shard_map/encoder_layer/pallas_call | solution.py:373
  96.4 2.3 %copy.13 = bf16[512,1024]{1,0:T(8,128)(2,1)} copy(bf16[512,1024]{1,0:T(8,128)(2,1)} %encoder_layer.1) | data formatting | bytes 2097152

commit v7 on v6

--- a/solution.py
+++ b/solution.py
@@ -180,11 +180,12 @@
     normed[...] = rms_scale(tokens_ref[...].astype(jnp.float32), gain_attn_ref[...]).astype(
         jnp.bfloat16
     )
-    for phase in (0, 1):
-        for chunk in chunks:
-            for piece in chunk:
-                piece.arrive(phase)
-                piece.open(phase + 1)
+    for turn in range(len(chunks) + 1):
+        for phase, number in ((0, turn), (1, turn - 1)):
+            if 0 <= number < len(chunks):
+                for piece in chunks[number]:
+                    piece.arrive(phase)
+                    piece.open(phase + 1)
 
     row_ids = lax.broadcasted_iota(jnp.int32, (seq_len, seq_len), 0)
     col_ids = lax.broadcasted_iota(jnp.int32, (seq_len, seq_len), 1)

time: 98.8 us -> 109 us (1.10)
  Pallas kernels: 96.3 us -> 106 us
    pallas_call x1, Pallas kernels: 96.3 us -> 106 us  [shards(): pl.pallas_call(layer_kernel, out_shape=jax.ShapeDtypeStruct((seq_len, wid...]
where the time goes in v7:
time: 109 us; the launch traced here: 108 us
  Pallas kernels  106 us (97%)
  local copies, waits for them, and re-layouts  2.26 us (2%)
    pallas_call x1, Pallas kernels, shards(): pl.pallas_call(layer_kernel, out_shape=jax.ShapeDtypeStruct((seq_len, wid...  106 us
    unnamed x1, local copies, waits for them, and re-layouts  2.26 us

profile of v7, /device:TPU:1, one launch (start us, length us, event | category | flops | bytes accessed | tf_op | source)
XLA Modules:
  0.0 108.2 jit_solution(7062771076269902724)
XLA Ops:
  0.0 105.9 %encoder_layer.1 = bf16[512,1024]{1,0:T(8,128)(2,1)} custom-call(s32[32]{0:T(128)} %swap_ref.1, bf16[512,1024]{1,0:T(8,128)(2,1)} %tokens_hbm.1, s32[1,512]{1,0:T(1,128)} %bitcast.2, bf16[8,3072]{1,0:T(8,128)(2,1)} %qkv_ref.1, bf16[8,1024]{1,0:T(8,128)(2,1)} %out_ref.1, bf16[1024]{0:T(1024)(128)(2,1)} %gain_attn_ref.1, bf16[1024]{0:T(1024)(128)(2,1)} %gain_expert_ref.1, ...), custom_call_target="tpu_custom_call" | custom-call | tf_op jit(solution)/shard_map/encoder_layer/pallas_call | solution.py:374
  105.9 2.3 %copy.13 = bf16[512,1024]{1,0:T(8,128)(2,1)} copy(bf16[512,1024]{1,0:T(8,128)(2,1)} %encoder_layer.1) | data formatting | bytes 2097152

commit v8 on v6

--- a/solution.py
+++ b/solution.py
@@ -184,7 +184,11 @@
         for chunk in chunks:
             for piece in chunk:
                 piece.arrive(phase)
-                piece.open(phase + 1)
+                if phase == 0:
+                    piece.open(1)
+    for chunk in chunks[:2]:
+        for piece in chunk:
+            piece.open(2)
 
     row_ids = lax.broadcasted_iota(jnp.int32, (seq_len, seq_len), 0)
     col_ids = lax.broadcasted_iota(jnp.int32, (seq_len, seq_len), 1)
@@ -208,6 +212,10 @@
             piece.arrive(2)
             piece.hand_over()
 
+    def open_last(number):
+        for piece in chunks[number] if number < len(chunks) else ():
+            piece.open(2)
+
     def head_step(head, carry):
         lane = lax.broadcasted_iota(jnp.int32, (1, heads_wide), 1)
         size = width // HEADS
@@ -226,6 +234,7 @@
         return carry
 
     hand_over(chunks[0])
+    open_last(2)
     per_group = HEADS // GROUPS
     scale = (width // HEADS) ** -0.5
     for g in range(GROUPS):
@@ -239,6 +248,7 @@
             target[...] = product * jnp.bfloat16(scale) if n == 0 else product
         summed[...] = jnp.zeros_like(summed)
         hand_over(chunks[g + 1])
+        open_last(g + 3)
         lax.fori_loop(0, per_group, head_step, 0)
         context[:, g * heads_wide : (g + 1) * heads_wide] = summed[...].astype(jnp.bfloat16)
 

time: 98.8 us -> 101 us (1.022)
  Pallas kernels: 96.3 us -> 99 us
    pallas_call x1, Pallas kernels: 96.3 us -> 99 us  [shards(): pl.pallas_call(layer_kernel, out_shape=jax.ShapeDtypeStruct((seq_len, wid...]
where the time goes in v8:
time: 101 us
  Pallas kernels  99 us (98%)
  local copies, waits for them, and re-layouts  2.26 us (2%)
    pallas_call x1, Pallas kernels, shards(): pl.pallas_call(layer_kernel, out_shape=jax.ShapeDtypeStruct((seq_len, wid...  99 us
    unnamed x1, local copies, waits for them, and re-layouts  2.26 us

profile of v8, /device:TPU:1, one launch (start us, length us, event | category | flops | bytes accessed | tf_op | source)
XLA Modules:
  0.0 101.3 jit_solution(9648032256896674052)
XLA Ops:
  0.0 99.0 %encoder_layer.1 = bf16[512,1024]{1,0:T(8,128)(2,1)} custom-call(s32[32]{0:T(128)} %swap_ref.1, bf16[512,1024]{1,0:T(8,128)(2,1)} %tokens_hbm.1, s32[1,512]{1,0:T(1,128)} %bitcast.2, bf16[8,3072]{1,0:T(8,128)(2,1)} %qkv_ref.1, bf16[8,1024]{1,0:T(8,128)(2,1)} %out_ref.1, bf16[1024]{0:T(1024)(128)(2,1)} %gain_attn_ref.1, bf16[1024]{0:T(1024)(128)(2,1)} %gain_expert_ref.1, ...), custom_call_target="tpu_custom_call" | custom-call | tf_op jit(solution)/shard_map/encoder_layer/pallas_call | solution.py:383
  99.0 2.3 %copy.13 = bf16[512,1024]{1,0:T(8,128)(2,1)} copy(bf16[512,1024]{1,0:T(8,128)(2,1)} %encoder_layer.1) | data formatting | bytes 2097152
